TPU v7x, 512 devices: a whole 4x4x16 slice. The times are simulated.
512 devices in a mesh: row: 8 (over x, core), col: 64 (over z, y).
Axes of the slice: x: 4, y: 4, z: 16, core: 2. Of those that a mesh axis runs over, the one named last changes fastest.
Arguments:
- impedance: bfloat16 [2, 8192, 65536], P(None, 'col', 'row'), may hold values from -0.015625 to 0.015625
- tile_scale: float32 [512, 128], P('col', 'row'), may hold values from 0.5 to 2
- krylov_block: bfloat16 [65536, 128], P(('row', 'col')), may hold values from -6 to 6
- prior_basis: float32 [8192, 512], P(('col', 'row'))
Outputs:
- coefficients: float32 [256, 128], replicated
- new_basis: float32 [8192, 128], P(('col', 'row'))
All inputs are finite; a program needn't handle non-finite values.
Results may differ from a plain program's by a relative error of at most 0.0003.
Values may be sent and summed in bfloat16 or wider, within the bound.
No kernel may reach another device: no remote copies, remote signals or barrier semaphores. Data moves between devices by JAX's collectives and lax.ppermute only.
A program may use at most 64 MiB of HBM per device.

v0:
```python
import jax
import jax.numpy as jnp
from jax import lax
from jax.sharding import PartitionSpec as P

PRIOR_BLOCKS = 4


def split_blocks(matrix, blocks):
    row_count = matrix.shape[0]
    columns = matrix.shape[1] // (2 * blocks)
    shaped = matrix.reshape(row_count, blocks, 2, columns)
    return (
        shaped[:, :, 0, :].reshape(row_count, blocks * columns),
        shaped[:, :, 1, :].reshape(row_count, blocks * columns),
    )


def inner_sum(left, right):
    return jnp.einsum("ra,rb->ab", left, right, precision=lax.Precision.HIGHEST)


def apply_basis(matrix, vector):
    return jnp.dot(matrix, vector, precision=lax.Precision.HIGHEST)


def combine_complex(running, angles):
    real_part = running[0][:, :angles] - running[1][:, angles:]
    imag_part = running[0][:, angles:] + running[1][:, :angles]
    return (real_part, imag_part)


def local_coefficients(summed, prior_rows):
    angles = summed.shape[1] // 2
    y_real = summed[:, :angles]
    y_imag = summed[:, angles:]
    basis_real, basis_imag = split_blocks(prior_rows, PRIOR_BLOCKS)
    coeff_local = jnp.concatenate(
        [
            inner_sum(basis_real, y_real) + inner_sum(basis_imag, y_imag),
            inner_sum(basis_real, y_imag) - inner_sum(basis_imag, y_real),
        ],
        1,
    )
    return coeff_local


def residual_parts(summed, prior_rows, coeffs):
    angles = summed.shape[1] // 2
    y_real = summed[:, :angles]
    y_imag = summed[:, angles:]
    basis_real, basis_imag = split_blocks(prior_rows, PRIOR_BLOCKS)
    coeff_real = coeffs[:, :angles]
    coeff_imag = coeffs[:, angles:]
    resid_real = y_real - (
        apply_basis(basis_real, coeff_real) - apply_basis(basis_imag, coeff_imag)
    )
    resid_imag = y_imag - (
        apply_basis(basis_real, coeff_imag) + apply_basis(basis_imag, coeff_real)
    )
    return (resid_real, resid_imag)


def scaled_rows(resid_real, resid_imag, squares, total_rows):
    factor = 1.0 / jnp.sqrt(squares / total_rows + 1e-06)
    return jnp.concatenate([resid_real * factor[None, :], resid_imag * factor[None, :]], 1)


def per_device(impedance, tile_scale, krylov_block, prior_basis):
    gathered = lax.all_gather(krylov_block, "col", axis=0, tiled=True)
    tiles = tile_scale.shape[1]
    tile_width = gathered.shape[0] // tiles
    tile_height = impedance.shape[1] // tile_scale.shape[0]
    pieces = impedance.reshape(2, impedance.shape[1], tiles, tile_width)
    entries = gathered.reshape(tiles, tile_width, gathered.shape[1])
    products = jnp.einsum("arjc,jcb->jarb", pieces, entries, preferred_element_type=jnp.float32)
    scales = jnp.repeat(tile_scale, tile_height, axis=0).T
    running = jnp.sum(products * scales[:, None, :, None], axis=0)
    angles = gathered.shape[1] // 2
    y_real, y_imag = combine_complex(running, angles)
    partials = jnp.concatenate([y_real, y_imag], 1)
    summed = lax.psum_scatter(partials, "row", scatter_dimension=0, tiled=True)
    coefficients = lax.psum(local_coefficients(summed, prior_basis), ("row", "col"))
    resid_real, resid_imag = residual_parts(summed, prior_basis, coefficients)
    squares = lax.psum(
        jnp.sum(resid_real * resid_real + resid_imag * resid_imag, axis=0), ("row", "col")
    )
    total_rows = summed.shape[0] * lax.axis_size("row") * lax.axis_size("col")
    new_basis = scaled_rows(resid_real, resid_imag, squares, total_rows)
    return (coefficients, new_basis)


def solution(mesh):
    return jax.shard_map(
        per_device,
        mesh=mesh,
        in_specs=(
            P(None, "col", "row"),
            P("col", "row"),
            P(("row", "col"), None),
            P(("col", "row"), None),
        ),
        out_specs=(P(), P(("col", "row"), None)),
        check_vma=False,
    )
```

profile of v0, /device:TPU:1, one launch (start us, length us, event | category | flops | bytes accessed | tf_op | source)
XLA Modules:
  0.0 763.1 jit_solution(16431430032423529162)
XLA Ops:
  7.2 0.0 all-gather.2.cloned.1.call-start
  7.2 0.7 all-gather.2.cloned.1.call-update
  7.9 0.0 reduce-scatter.2.cloned.1.call-start
  7.9 0.8 copy.7
  8.7 0.1 broadcast_in_dim.2
  8.8 0.1 reshape.21
  8.9 139.5 %all-gather.2.cloned.1.call-done = bf16[8192,128]{1,0:T(8,128)(2,1)} async-done(((bf16[128,128]{1,0:T(8,128)(2,1)}), bf16[8192,128]{1,0:T(8,128)(2,1)}) %all-gather.2.cloned.1.call-update) | async-done | bytes 2097168 | tf_op jit(solution)/shard_map/all_gather | solution.py:70
  148.4 0.0 copy-start
  148.4 4.1 multiply_reduce_fusion
  152.6 0.1 slice_subtract_fusion
  152.7 0.7 pad_maximum_fusion.1
  153.4 0.0 reduce-scatter.2.cloned.1.call-update
  153.4 0.0 all-reduce.2.cloned.1.call-start
  153.5 0.0 copy-done
  153.5 0.1 reshape.22
  153.6 0.2 slice_reduce_fusion
  153.8 0.1 reshape_squeeze.9
  153.9 0.1 reshape_squeeze.8
  153.9 40.7 %reduce-scatter.2.cloned.1.call-done = f32[16,128]{1,0:T(8,128)} async-done(((f32[128,128]{1,0:T(8,128)}), f32[16,128]{1,0:T(8,128)}) %reduce-scatter.2.cloned.1.call-update) | async-done | bytes 8208 | tf_op jit(solution)/shard_map/reduce_scatter | solution.py:82
  194.7 1.0 fusion.17
  195.7 0.9 fusion.21
  196.7 0.9 fusion.5
  197.6 1.0 fusion.6
  198.7 0.7 pad_maximum_fusion
  199.3 0.0 all-reduce.2.cloned.1.call-update
  199.4 451.0 %all-reduce.2.cloned.1.call-done = f32[256,128]{0,1:T(8,128)} async-done(((f32[256,128]{0,1:T(8,128)}), f32[256,128]{0,1:T(8,128)}) %all-reduce.2.cloned.1.call-update) | async-done | bytes 131088 | tf_op jit(solution)/shard_map/psum | solution.py:83
  650.4 1.0 fusion.11
  651.4 1.0 fusion.15
  652.4 1.0 fusion.10
  653.4 1.0 add_reduce_fusion
  654.5 99.7 %psum.15 = f32[64]{0:T(128)S(1)} all-reduce(f32[64]{0:T(128)S(1)} %get-tuple-element.12), channel_id=1, replica_groups=mesh['row'=8,'col'=64] {'row','col'}, use_global_device_ids=true, to_apply=%region_4.0 | all-reduce | flops 64 | bytes 512 | tf_op jit(solution)/shard_map/psum | solution.py:85
  754.2 0.7 pad_maximum_fusion.2
  754.9 1.7 copy.8
  (3 shorter events, 0.0 us)
Async XLA Ops:
  7.2 141.2 %all-gather.2.cloned.1.call-start = ((), (), s32[]{:S(2)}) async-start(), calls=%async_computation.1 | async-start | bytes 2129920 | tf_op jit(solution)/shard_map/all_gather | solution.py:70
  7.9 186.8 %reduce-scatter.2.cloned.1.call-start = ((), (), s32[]{:S(2)}) async-start(), calls=%async_computation.2 | async-start | bytes 73728 | tf_op jit(solution)/shard_map/reduce_scatter | solution.py:82
  148.4 5.0 copy-start
  153.4 497.0 %all-reduce.2.cloned.1.call-start = ((), (), s32[]{:S(2)}) async-start(), calls=%async_computation.3 | async-start | bytes 262144 | tf_op jit(solution)/shard_map/psum | solution.py:83
Sparse Core Ops, SparseCore 0:
  10.9 137.4 all-gather.1
  153.5 41.1 reduce-scatter.1
  201.6 448.7 all-reduce.1
where the time goes:
time: 764 us; the launch traced here: 763 us
  waiting for transfers between devices  632 us (83%)
  blocking collectives  99.7 us (13%)
  between operations  13.8 us (2%)
  matrix products  12.1 us (2%)
    psum x1, waiting for transfers between devices, per_device(): lax.psum(local_coefficients(summed, prior_basis), ('row', 'col'))  451 us
    all_gather x1, waiting for transfers between devices, per_device(): gathered = lax.all_gather(krylov_block, 'col', axis=0, tiled=True)  140 us
    psum x1, blocking collectives, per_device(): lax.psum(jnp.sum(resid_real * resid_real + resid_imag * resid_imag, axis=...  99.7 us
    reduce_scatter x1, waiting for transfers between devices, per_device(): summed = lax.psum_scatter(partials, 'row', scatter_dimension=0, tiled=True)  40.7 us
  transfers between devices with their start and end apart: 3, of which 3 were waited for; matrix products, arithmetic and copies ran while one was open for 0% of the time, Pallas kernels for 0%

commit v1 on v0

v1 whole, which is shorter than its diff:
```python
import jax
import jax.numpy as jnp
from jax import lax
from jax.sharding import Mesh, PartitionSpec as P

ROW = ("x", "core")
COL = ("z", "y")
PLANE = ("x", "core", "y")
HIGHEST = lax.Precision.HIGHEST


def spread(block, axes):
    size = lax.axis_size(axes)
    copies = jnp.broadcast_to(block[None], (size,) + block.shape)
    return lax.all_to_all(copies, axes, 0, 0, tiled=True)


def scatter_sum(block, axes):
    size = lax.axis_size(axes)
    parts = block.reshape((size, block.shape[0] // size) + block.shape[1:])
    return jnp.sum(lax.all_to_all(parts, axes, 0, 0, tiled=True), axis=0)


def slab_product(impedance, tile_scale, entries):
    ys, zs, depth, columns = entries.shape
    rows = impedance.shape[1]
    tile_height = rows // tile_scale.shape[0]
    pieces = impedance.reshape(2, rows, zs, ys, depth)
    products = jnp.einsum("arzyi,yzib->zarb", pieces, entries, preferred_element_type=jnp.float32)
    scales = jnp.repeat(tile_scale, tile_height, axis=0).T
    running = jnp.sum(products * scales[:, None, :, None], axis=0)
    half = columns // 2
    real = running[0][:, :half] - running[1][:, half:]
    imag = running[0][:, half:] + running[1][:, :half]
    return jnp.concatenate([real, imag], 1)


def project(basis, product, blocks):
    half = product.shape[1] // 2
    inner = jnp.einsum("ra,rb->ab", basis, product, precision=HIGHEST)
    inner = inner.reshape(blocks, 2, half, 2 * half)
    from_real, from_imag = inner[:, 0], inner[:, 1]
    real = from_real[..., :half] + from_imag[..., half:]
    imag = from_real[..., half:] - from_imag[..., :half]
    return jnp.concatenate([real, imag], -1).reshape(blocks * half, 2 * half)


def subtract(basis, product, coefficients, blocks):
    half = product.shape[1] // 2
    shaped = coefficients.reshape(blocks, half, 2 * half)
    turned = jnp.concatenate([-shaped[..., half:], shaped[..., :half]], -1)
    both = jnp.stack([shaped, turned], 1).reshape(2 * blocks * half, 2 * half)
    return product - jnp.dot(basis, both, precision=HIGHEST)


def per_device(impedance, tile_scale, krylov_block, prior_basis):
    columns = krylov_block.shape[1]
    half = columns // 2
    blocks = prior_basis.shape[1] // columns
    with jax.named_scope("entries_z"):
        along_z = spread(krylov_block, "z")
    with jax.named_scope("entries_y"):
        entries = spread(along_z, "y")
    with jax.named_scope("slab"):
        partial = slab_product(impedance, tile_scale, entries)
    with jax.named_scope("product_rows"):
        product = scatter_sum(partial, ROW)
    with jax.named_scope("project"):
        local = project(prior_basis, product, blocks)
    with jax.named_scope("coefficients_plane"):
        chunk = scatter_sum(local, PLANE)
    with jax.named_scope("coefficients_z"):
        chunk = jnp.sum(spread(chunk, "z"), axis=0)
    with jax.named_scope("coefficients_all"):
        coefficients = spread(chunk, PLANE).reshape(blocks * half, columns)
    with jax.named_scope("residual"):
        residual = subtract(prior_basis, product, coefficients, blocks)
    with jax.named_scope("squares"):
        sums = jnp.sum(residual * residual, axis=0)
        sums = jnp.sum(spread(sums, ("x", "y")), axis=0)
        sums = jnp.sum(spread(sums, ("core", "z")), axis=0)
        squares = sums[:half] + sums[half:]
    with jax.named_scope("scale"):
        total_rows = prior_basis.shape[0] * lax.axis_size(ROW + COL)
        factor = 1.0 / jnp.sqrt(squares / total_rows + 1e-06)
        new_basis = residual * jnp.concatenate([factor, factor])[None, :]
    return (coefficients, new_basis)


def solution(mesh):
    rows = 4 if mesh.shape["row"] % 4 == 0 else 1
    devices = mesh.devices.reshape(rows, mesh.shape["row"] // rows, mesh.shape["col"] // 4, 4)
    fine = Mesh(devices, ("x", "core", "z", "y"))
    return jax.shard_map(
        per_device,
        mesh=fine,
        in_specs=(
            P(None, COL, ROW),
            P(COL, ROW),
            P(ROW + COL, None),
            P(COL + ROW, None),
        ),
        out_specs=(P(), P(COL + ROW, None)),
        check_vma=False,
    )
```

time: 764 us -> 167 us (0.22)
  waiting for transfers between devices: 632 us -> 22.5 us
  blocking collectives: 99.7 us -> 113 us
  between operations: 13.8 us -> 0.78 us
  starting transfers between devices: 0.12 us -> 10.3 us
  local copies, waits for them, and re-layouts: 3.07 us -> 12.2 us
    psum x1 -> x0, waiting for transfers between devices: 451 us -> none  [per_device(): lax.psum(local_coefficients(summed, prior_basis), ('row', 'col'))]
    all_gather x1 -> x0, waiting for transfers between devices: 140 us -> none  [per_device(): gathered = lax.all_gather(krylov_block, 'col', axis=0, tiled=True)]
    all_to_all x0 -> x6, blocking collectives: none -> 113 us  [the longest x4 84.1 us: spread(): return lax.all_to_all(copies, axes, 0, 0, tiled=True)]
    psum x1 -> x0, blocking collectives: 99.7 us -> none  [per_device(): lax.psum(jnp.sum(resid_real * resid_real + resid_imag * resid_imag, axis=...]
    reduce_scatter x1 -> x0, waiting for transfers between devices: 40.7 us -> none  [per_device(): summed = lax.psum_scatter(partials, 'row', scatter_dimension=0, tiled=True)]
    all_to_all x0 -> x2, waiting for transfers between devices: none -> 22.5 us  [spread(): return lax.all_to_all(copies, axes, 0, 0, tiled=True)]
    all_to_all x0 -> x2, starting transfers between devices: none -> 10.3 us  [spread(): return lax.all_to_all(copies, axes, 0, 0, tiled=True)]
  transfers between devices with their start and end apart: 3 -> 2, of which waited for: 3 -> 2; matrix products, arithmetic and copies ran while one was open for 0% -> 5% of each run, Pallas kernels for 0% -> 0%
where the time goes in v1:
time: 167 us; the launch traced here: 166 us
  blocking collectives  113 us (68%)
  waiting for transfers between devices  22.5 us (13%)
  local copies, waits for them, and re-layouts  12.2 us (7%)
  starting transfers between devices  10.3 us (6%)
  matrix products  5.58 us (3%)
    all_to_all x4, blocking collectives, spread(): return lax.all_to_all(copies, axes, 0, 0, tiled=True)  84.1 us
    all_to_all x2, blocking collectives, scatter_sum(): return jnp.sum(lax.all_to_all(parts, axes, 0, 0, tiled=True), axis=0)  29 us
    all_to_all x2, waiting for transfers between devices, spread(): return lax.all_to_all(copies, axes, 0, 0, tiled=True)  22.5 us
    all_to_all x2, starting transfers between devices, spread(): return lax.all_to_all(copies, axes, 0, 0, tiled=True)  10.3 us
    reshape x1, local copies, waits for them, and re-layouts, slab_product(): pieces = impedance.reshape(2, rows, zs, ys, depth)  7.72 us
    dot_general x1, matrix products, slab_product(): jnp.einsum('arzyi,yzib->zarb', pieces, entries, preferred_element_type=jn...  4.89 us
    broadcast_in_dim x6, local copies, waits for them, and re-layouts, spread(): copies = jnp.broadcast_to(block[None], (size,) + block.shape)  3.4 us
  transfers between devices with their start and end apart: 2, of which 2 were waited for; matrix products, arithmetic and copies ran while one was open for 5% of the time, Pallas kernels for 0%

profile of v1, /device:TPU:1, one launch (start us, length us, event | category | flops | bytes accessed | tf_op | source)
XLA Modules:
  0.0 165.9 jit_solution(13383685927725634111)
XLA Ops:
  0.6 0.0 copy-start
  0.6 0.9 broadcast_in_dim.14
  1.5 38.4 %all_to_all.42 = bf16[16,128,128]{2,1,0:T(8,128)(2,1)S(1)} all-to-all(bf16[16,128,128]{2,1,0:T(8,128)(2,1)S(1)} %broadcast_in_dim.14), channel_id=1, replica_groups=mesh['x'=4,'core'=2,'z'=16,'y'=4] {'z'}, dimensions={0} | all-to-all | bytes 1048576 | tf_op jit(solution)/shard_map/entries_z/all_to_all | solution.py:15
  39.9 1.9 %broadcast_in_dim.15 = bf16[4,16,128,128]{3,2,1,0:T(8,128)(2,1)} broadcast(bf16[16,128,128]{2,1,0:T(8,128)(2,1)S(1)} %all_to_all.42), dimensions={1,2,3} | broadcast | bytes 2621440 | tf_op jit(solution)/shard_map/entries_y/broadcast_in_dim | solution.py:14
  41.8 0.0 copy-start.1
  41.8 4.3 %all-to-all-start.1 = ((bf16[4,16,128,128]{3,2,1,0:T(8,128)(2,1)}), bf16[4,16,128,128]{3,2,1,0:T(8,128)(2,1)S(1)}, u32[]{:S(2)}, u32[]{:S(2)}) async-start(bf16[4,16,128,128]{3,2,1,0:T(8,128)(2,1)} %broadcast_in_dim.15), calls=%async_computation.1 | async-start | bytes 4194304 | tf_op jit(solution)/shard_map/entries_y/all_to_all | solution.py:15
  46.1 0.0 copy-done.1
  46.1 0.1 copy.25
  46.2 0.1 broadcast_in_dim.16
  46.3 0.1 reshape.50
  46.3 7.7 %reshape.49 = bf16[2,128,16,4,128]{4,3,2,1,0:T(4,128)(2,1)} reshape(bf16[2,128,8192]{2,1,0:T(8,128)(2,1)} %param.4) | data formatting | bytes 8388608 | tf_op jit(solution)/shard_map/slab/reshape | solution.py:28
  54.1 10.6 %all-to-all-done.1 = bf16[4,16,128,128]{3,2,1,0:T(8,128)(2,1)S(1)} async-done(((bf16[4,16,128,128]{3,2,1,0:T(8,128)(2,1)}), bf16[4,16,128,128]{3,2,1,0:T(8,128)(2,1)S(1)}, u32[]{:S(2)}, u32[]{:S(2)}) %all-to-all-start.1) | async-done | bytes 2097184 | tf_op jit(solution)/shard_map/entries_y/all_to_all | solution.py:15
  64.7 4.9 %fusion.2 = f32[2,128,128]{2,1,0:T(8,128)S(1)} fusion(f32[16,128]{1,0:T(8,128)S(1)} %bitcast.52, bf16[2,128,16,4,128]{4,3,2,1,0:T(4,128)(2,1)} %reshape.49, bf16[4,16,128,128]{3,2,1,0:T(8,128)(2,1)S(1)} %all-to-all-done.1), kind=kOutput, calls=%fused_computation.3 | convolution fusion | flops 537886720 | bytes 6430720 | tf_op jit(solution)/shard_map/slab/arzyi,yzib->zarb/dot_general | solution.py:29
  69.6 0.1 slice_subtract_fusion.1
  69.7 0.1 pad_maximum_fusion.2
  69.8 17.7 %all_to_all.43 = f32[8,16,128]{2,1,0:T(8,128)S(1)} all-to-all(f32[8,16,128]{2,1,0:T(8,128)S(1)} %bitcast.49), channel_id=1, replica_groups=mesh['x'=4,'core'=2,'z'=16,'y'=4] {'x','core'}, dimensions={0} | all-to-all | bytes 131072 | tf_op jit(solution)/shard_map/product_rows/all_to_all | solution.py:21
  87.5 0.0 copy-done
  87.5 0.4 convolution_bitcast_fusion
  87.9 0.1 copy.26
  88.1 0.1 slice_add_fusion
  88.2 0.1 pad_maximum_fusion.1
  88.3 11.4 %all_to_all.44 = f32[32,8,128]{2,1,0:T(8,128)S(1)} all-to-all(f32[32,8,128]{2,1,0:T(8,128)S(1)} %bitcast.48), channel_id=1, replica_groups=mesh['x'=4,'core'=2,'z'=16,'y'=4] {'x','core','y'}, dimensions={0} | all-to-all | bytes 262144 | tf_op jit(solution)/shard_map/coefficients_plane/all_to_all | solution.py:21
  99.7 23.9 %all_to_all.45 = f32[16,8,128]{2,1,0:T(8,128)S(1)} all-to-all(f32[16,8,128]{2,1,0:T(8,128)S(1)} %broadcast_in_dim.17), channel_id=1, replica_groups=mesh['x'=4,'core'=2,'z'=16,'y'=4] {'z'}, dimensions={0} | all-to-all | bytes 131072 | tf_op jit(solution)/shard_map/coefficients_z/all_to_all | solution.py:15
  123.7 12.9 %all_to_all.46 = f32[32,8,128]{2,1,0:T(8,128)S(1)} all-to-all(f32[32,8,128]{2,1,0:T(8,128)S(1)} %broadcast_in_dim.18), channel_id=1, replica_groups=mesh['x'=4,'core'=2,'z'=16,'y'=4] {'x','core','y'}, dimensions={0} | all-to-all | bytes 262144 | tf_op jit(solution)/shard_map/coefficients_all/all_to_all | solution.py:15
  136.5 0.1 slice_negate_fusion
  136.6 0.1 maximum_bitcast_fusion
  136.8 0.3 multiply_reduce_fusion
  137.1 9.0 %all_to_all.47 = f32[16,1,128]{2,1,0:T(1,128)S(1)} all-to-all(f32[16,1,128]{2,1,0:T(1,128)S(1)} %broadcast_in_dim.19), channel_id=1, replica_groups=mesh['x'=4,'core'=2,'z'=16,'y'=4] {'x','y'}, dimensions={0} | all-to-all | bytes 16384 | tf_op jit(solution)/shard_map/squares/all_to_all | solution.py:15
  146.0 0.6 broadcast_in_dim.20
  146.7 6.0 %all-to-all-start.7 = ((f32[32,1,128]{2,1,0:T(1,128)}), f32[32,1,128]{2,1,0:T(1,128)S(1)}, u32[]{:S(2)}, u32[]{:S(2)}) async-start(f32[32,1,128]{2,1,0:T(1,128)} %broadcast_in_dim.20), calls=%async_computation.7 | async-start | bytes 32768 | tf_op jit(solution)/shard_map/squares/all_to_all | solution.py:15
  152.6 11.9 %all-to-all-done.7 = f32[32,1,128]{2,1,0:T(1,128)S(1)} async-done(((f32[32,1,128]{2,1,0:T(1,128)}), f32[32,1,128]{2,1,0:T(1,128)S(1)}, u32[]{:S(2)}, u32[]{:S(2)}) %all-to-all-start.7) | async-done | bytes 16416 | tf_op jit(solution)/shard_map/squares/all_to_all | solution.py:15
  164.5 0.1 add_rsqrt_fusion
  164.6 0.1 pad_maximum_fusion.3
  164.7 0.6 broadcast_multiply_fusion
  165.3 0.7 copy.44
  (11 shorter events, 0.2 us)
Async XLA Ops:
  0.6 86.8 %copy-start = (f32[16,512]{1,0:T(8,128)S(1)}, f32[16,512]{1,0:T(8,128)}, u32[]{:S(2)}) copy-start(f32[16,512]{1,0:T(8,128)} %param.7) | copy-start | bytes 98308
  41.8 4.3 %copy-start.1 = (f32[8,16]{1,0:T(8,128)S(1)}, f32[8,16]{1,0:T(8,128)}, u32[]{:S(2)}) copy-start(f32[8,16]{1,0:T(8,128)} %param.5) | copy-start | bytes 1540
  41.8 22.9 %all-to-all-start.1 = ((bf16[4,16,128,128]{3,2,1,0:T(8,128)(2,1)}), bf16[4,16,128,128]{3,2,1,0:T(8,128)(2,1)S(1)}, u32[]{:S(2)}, u32[]{:S(2)}) async-start(bf16[4,16,128,128]{3,2,1,0:T(8,128)(2,1)} %broadcast_in_dim.15), calls=%async_computation.1 | async-start | bytes 4194304 | tf_op jit(solution)/shard_map/entries_y/all_to_all | solution.py:15
  146.7 17.8 %all-to-all-start.7 = ((f32[32,1,128]{2,1,0:T(1,128)}), f32[32,1,128]{2,1,0:T(1,128)S(1)}, u32[]{:S(2)}, u32[]{:S(2)}) async-start(f32[32,1,128]{2,1,0:T(1,128)} %broadcast_in_dim.20), calls=%async_computation.7 | async-start | bytes 32768 | tf_op jit(solution)/shard_map/squares/all_to_all | solution.py:15

commit v2 on v1

v2 whole, which is shorter than its diff:
```python
import functools

import jax
import jax.numpy as jnp
from jax import lax
from jax.experimental import pallas as pl
from jax.experimental.pallas import tpu as pltpu
from jax.sharding import Mesh, PartitionSpec as P

ROW = ("x", "core")
COL = ("z", "y")
PLANE = ("x", "core", "y")
HIGHEST = lax.Precision.HIGHEST


def spread(block, axes):
    size = lax.axis_size(axes)
    copies = jnp.broadcast_to(block[None], (size,) + block.shape)
    return lax.all_to_all(copies, axes, 0, 0, tiled=True)


def ring_gather(block, axis):
    size = lax.axis_size(axis)
    me = lax.axis_index(axis)
    stacked = jnp.zeros((size,) + block.shape, block.dtype)
    for step in range(size):
        pairs = [(member, (member + step) % size) for member in range(size)]
        arrived = lax.ppermute(block, axis, pairs) if step else block
        owner = lax.rem(me - step + size, size)
        stacked = lax.dynamic_update_index_in_dim(stacked, arrived, owner, 0)
    return stacked


def turn(block, first, second):
    half = block.shape[1] // 2
    lanes = lax.broadcasted_iota(jnp.int32, block.shape, 1)
    return pltpu.roll(block, half, 1) * jnp.where(lanes < half, first, second)


def slab_kernel(chunks, impedance, scales, entries, basis, out, held, sems):
    rows, columns = scales.shape[0], entries.shape[3]
    ys, zs, depth, _ = entries.shape
    width = ys * depth
    members, height, _ = out.shape
    share = rows // members
    span = zs * width // chunks
    copies = []
    for chunk in range(chunks):
        part = pl.ds(chunk * span, span)
        copies.append(pltpu.make_async_copy(impedance.at[:, :, part], held.at[:, :, part], sems.at[chunk]))
        copies[-1].start()
    running = jnp.zeros((2, rows, columns), jnp.float32)
    for tile in range(zs):
        if tile % (zs // chunks) == 0:
            copies[tile // (zs // chunks)].wait()
        piece = held[:, :, tile * width : (tile + 1) * width].reshape(2 * rows, width)
        block = entries[:, tile].reshape(width, columns)
        product = jnp.dot(piece, block, preferred_element_type=jnp.float32)
        running += product.reshape(2, rows, columns) * scales[:, tile : tile + 1][None]
    partial = running[0] + turn(running[1], -1.0, 1.0)
    inner = jnp.dot(basis[...], partial, precision=HIGHEST, preferred_element_type=jnp.float32)
    half = columns // 2
    inner = inner.reshape(-1, 2, half, columns)
    sums = inner[:, 0].reshape(-1, columns) + turn(inner[:, 1].reshape(-1, columns), 1.0, -1.0)
    out[:, : height - share, :] = sums.reshape(members, height - share, columns)
    for member in range(members):
        out[member, height - share :, :] = partial[member * share : (member + 1) * share]


def slab_sums(impedance, scales, entries, basis, members):
    rows = impedance.shape[1]
    columns = entries.shape[3]
    chunks = 4
    height = (basis.shape[0] // 2 + rows) // members
    vmem = pl.BlockSpec(memory_space=pltpu.VMEM)
    return pl.pallas_call(
        functools.partial(slab_kernel, chunks),
        out_shape=jax.ShapeDtypeStruct((members, height, columns), jnp.float32),
        in_specs=[pl.BlockSpec(memory_space=pltpu.HBM), vmem, vmem, vmem],
        out_specs=vmem,
        scratch_shapes=[pltpu.VMEM(impedance.shape, impedance.dtype), pltpu.SemaphoreType.DMA((chunks,))],
        compiler_params=pltpu.CompilerParams(vmem_limit_bytes=48 * 2**20),
        cost_estimate=pl.CostEstimate(
            flops=4 * impedance.shape[2] * rows * columns,
            bytes_accessed=2 * (impedance.size + entries.size),
            transcendentals=0,
        ),
    )(impedance, scales, entries, basis)


def residual_kernel(taken, basis, coefficients, residual, sums):
    members, height, columns = taken.shape
    count = coefficients.shape[0]
    half = columns // 2
    found = taken[:, : count // members, :].reshape(count, columns)
    product = taken[:, count // members :, :].reshape(residual.shape)
    coefficients[...] = found
    turned = turn(found, -1.0, 1.0)
    pair = [found.reshape(-1, 1, half, columns), turned.reshape(-1, 1, half, columns)]
    both = jnp.concatenate(pair, 1).reshape(2 * count, columns)
    rest = product - jnp.dot(basis[...], both, precision=HIGHEST, preferred_element_type=jnp.float32)
    residual[...] = rest
    sums[...] = jnp.broadcast_to(jnp.sum(rest * rest, axis=0, keepdims=True), sums.shape)


def plane_residual(taken, basis, copies):
    members, height, columns = taken.shape
    rows, width = basis.shape
    vmem = pl.BlockSpec(memory_space=pltpu.VMEM)
    shapes = [(width // 2, columns), (rows, columns), (copies, columns)]
    return pl.pallas_call(
        residual_kernel,
        out_shape=[jax.ShapeDtypeStruct(shape, jnp.float32) for shape in shapes],
        in_specs=[vmem, vmem],
        out_specs=[vmem] * 3,
        compiler_params=pltpu.CompilerParams(vmem_limit_bytes=24 * 2**20),
        cost_estimate=pl.CostEstimate(
            flops=12 * rows * width * columns,
            bytes_accessed=4 * (taken.size + basis.size + rows * columns),
            transcendentals=0,
        ),
    )(taken, basis)


def per_device(impedance, tile_scale, krylov_block, prior_basis):
    columns = krylov_block.shape[1]
    half = columns // 2
    width = prior_basis.shape[1]
    own_rows = prior_basis.shape[0]
    rows = impedance.shape[1]
    ys, zs, row_members, members = (lax.axis_size(axes) for axes in ("y", "z", ROW, PLANE))
    share = rows // members
    height = width // 2 // members
    with jax.named_scope("basis_pair"):
        pair = ring_gather(ring_gather(prior_basis, "y"), "core")
    with jax.named_scope("entries_z"):
        along_z = spread(krylov_block, "z")
    with jax.named_scope("entries_y"):
        along_z, pair = lax.optimization_barrier((along_z, pair))
        entries = spread(along_z, "y")
    with jax.named_scope("basis_plane"):
        gathered = ring_gather(pair, "x").reshape(row_members, ys, own_rows, width)
        here = lax.dynamic_index_in_dim(gathered, lax.axis_index("y"), 1, False).reshape(rows, width).T
        basis = gathered.reshape(row_members, ys, own_rows // share, share, width)
        basis = jnp.swapaxes(basis, 1, 2).reshape(members * ys * share, width)
        row, y = lax.axis_index(ROW).astype(jnp.int32), lax.axis_index("y").astype(jnp.int32)
        scales = jnp.repeat(tile_scale, rows // tile_scale.shape[0], axis=0)
        entries, here, basis, scales, row, y = lax.optimization_barrier((entries, here, basis, scales, row, y))
    with jax.named_scope("slab"):
        parts = slab_sums(impedance, scales, entries, here, members)
    with jax.named_scope("sums_plane"):
        taken = lax.all_to_all(parts, PLANE, 0, 0, tiled=True)
        chunk = jnp.sum(taken[:, :height], axis=0)
        product = jnp.sum(taken[:, height:].reshape(row_members, ys * share, columns), axis=0)
        chunk, product = lax.optimization_barrier((chunk, product))
    with jax.named_scope("coefficients_z"):
        chunk = jnp.sum(spread(chunk, "z"), axis=0)
    with jax.named_scope("gather_plane"):
        taken = spread(jnp.concatenate([chunk, product], 0), PLANE)
    with jax.named_scope("residual"):
        coefficients, residual, sums = plane_residual(taken, basis, zs)
        own = residual.reshape(row_members, own_rows // share, ys, share, columns)
        sizes = (1, own_rows // share, 1, share, columns)
        zero = jnp.int32(0)
        own = lax.dynamic_slice(own, (row, zero, y, zero, zero), sizes, allow_negative_indices=False)
        own = own.reshape(own_rows, columns)
        own, sums = lax.optimization_barrier((own, sums))
    with jax.named_scope("squares"):
        sums = jnp.sum(lax.all_to_all(sums, "z", 0, 0, tiled=True), axis=0)
        squares = sums[:half] + sums[half:]
    with jax.named_scope("scale"):
        total_rows = own_rows * lax.axis_size(ROW + COL)
        factor = 1.0 / jnp.sqrt(squares / total_rows + 1e-06)
        new_basis = own * jnp.concatenate([factor, factor])[None, :]
    return (coefficients, new_basis)


def solution(mesh):
    rows = 4 if mesh.shape["row"] % 4 == 0 else 1
    devices = mesh.devices.reshape(rows, mesh.shape["row"] // rows, mesh.shape["col"] // 4, 4)
    fine = Mesh(devices, ("x", "core", "z", "y"))
    return jax.shard_map(
        per_device,
        mesh=fine,
        in_specs=(
            P(None, COL, ROW),
            P(COL, ROW),
            P(ROW + COL, None),
            P(COL + ROW, None),
        ),
        out_specs=(P(), P(COL + ROW, None)),
        check_vma=False,
    )
```

time: 167 us -> 148 us (0.89)
  blocking collectives: 113 us -> 74 us
  starting transfers between devices: 10.3 us -> 45.4 us
  waiting for transfers between devices: 22.5 us -> 9.89 us
  matrix products: 5.58 us -> 0 us
  Pallas kernels: 0 us -> 4.9 us
    all_to_all x4 -> x2, blocking collectives: 84.1 us -> 35.8 us  [spread(): return lax.all_to_all(copies, axes, 0, 0, tiled=True)]
    ppermute x0 -> x7, starting transfers between devices: none -> 25.5 us  [ring_gather(): arrived = lax.ppermute(block, axis, pairs) if step else block]
    all_to_all x2, waiting for transfers between devices: 22.5 us -> 4.57 us  [spread(): return lax.all_to_all(copies, axes, 0, 0, tiled=True)]
    all_to_all x2, starting transfers between devices: 10.3 us -> 19.9 us  [spread(): return lax.all_to_all(copies, axes, 0, 0, tiled=True)]
    all_to_all x2, blocking collectives: 29 us -> 38.3 us  [the longest x1 24.5 us: per_device(): taken = lax.all_to_all(parts, PLANE, 0, 0, tiled=True)]
    dot_general x3 -> x0, matrix products: 5.58 us -> none  [the longest x1 4.89 us: slab_product(): jnp.einsum('arzyi,yzib->zarb', pieces, entries, preferred_element_type=jn...]
    ppermute x0 -> x7, waiting for transfers between devices: none -> 5.33 us  [ring_gather(): arrived = lax.ppermute(block, axis, pairs) if step else block]
    reshape x2, local copies, waits for them, and re-layouts: 7.81 us -> 2.65 us  [the longest x1 1.58 us: per_device(): basis = jnp.swapaxes(basis, 1, 2).reshape(members * ys * share, width)]
  transfers between devices with their start and end apart: 2 -> 9, of which waited for: 2 -> 5; matrix products, arithmetic and copies ran while one was open for 5% -> 5% of each run, Pallas kernels for 0% -> 0%
where the time goes in v2:
time: 148 us; the launch traced here: 147 us
  blocking collectives  74 us (50%)
  starting transfers between devices  45.4 us (31%)
  local copies, waits for them, and re-layouts  11 us (7%)
  waiting for transfers between devices  9.89 us (7%)
  Pallas kernels  4.9 us (3%)
    all_to_all x2, blocking collectives, spread(): return lax.all_to_all(copies, axes, 0, 0, tiled=True)  35.8 us
    ppermute x7, starting transfers between devices, ring_gather(): arrived = lax.ppermute(block, axis, pairs) if step else block  25.5 us
    all_to_all x1, blocking collectives, per_device(): taken = lax.all_to_all(parts, PLANE, 0, 0, tiled=True)  24.5 us
    all_to_all x2, starting transfers between devices, spread(): return lax.all_to_all(copies, axes, 0, 0, tiled=True)  19.9 us
    all_to_all x1, blocking collectives, per_device(): sums = jnp.sum(lax.all_to_all(sums, 'z', 0, 0, tiled=True), axis=0)  13.8 us
    ppermute x7, waiting for transfers between devices, ring_gather(): arrived = lax.ppermute(block, axis, pairs) if step else block  5.33 us
    all_to_all x2, waiting for transfers between devices, spread(): return lax.all_to_all(copies, axes, 0, 0, tiled=True)  4.57 us
    pallas_call x1, Pallas kernels, slab_sums(): pl.pallas_call(functools.partial(slab_kernel, chunks), out_shape=jax.Shap...  3.82 us
  transfers between devices with their start and end apart: 9, of which 5 were waited for; matrix products, arithmetic and copies ran while one was open for 5% of the time, Pallas kernels for 0%

profile of v2, /device:TPU:1, one launch (start us, length us, event | category | flops | bytes accessed | tf_op | source)
XLA Modules:
  0.0 147.1 jit_solution(2587905704921717959)
XLA Ops:
  0.6 1.6 %broadcast_in_dim.70 = bf16[16,128,128]{2,1,0:T(8,128)(2,1)} broadcast(bf16[128,128]{1,0:T(8,128)(2,1)} %param.6), dimensions={1,2} | broadcast | bytes 557056 | tf_op jit(solution)/shard_map/entries_z/broadcast_in_dim | solution.py:18
  2.3 15.7 %all-to-all-start = ((bf16[16,128,128]{2,1,0:T(8,128)(2,1)}), bf16[16,128,128]{2,1,0:T(8,128)(2,1)S(1)}, u32[]{:S(2)}, u32[]{:S(2)}) async-start(bf16[16,128,128]{2,1,0:T(8,128)(2,1)} %broadcast_in_dim.70), calls=%async_computation | async-start | bytes 1048576 | tf_op jit(solution)/shard_map/entries_z/all_to_all | solution.py:19
  18.0 3.2 %collective-permute-start = (f32[16,512]{1,0:T(8,128)}, f32[16,512]{1,0:T(8,128)S(1)}, u32[]{:S(2)}, u32[]{:S(2)}) collective-permute-start(f32[16,512]{1,0:T(8,128)} %param.7), channel_id=1, source_target_pairs={{0,1},{1,2},{2,3},{3,0},{4,5},{5,6},{6,7},{7,4},{8,9},{9,10},{10,1... | collective-permute-start | bytes 98312 | tf_op jit(solution)/shard_map/basis_pair/ppermute | solution.py:28
  21.2 4.5 %collective-permute-start.1 = (f32[16,512]{1,0:T(8,128)}, f32[16,512]{1,0:T(8,128)S(1)}, u32[]{:S(2)}, u32[]{:S(2)}) collective-permute-start(f32[16,512]{1,0:T(8,128)} %param.7), channel_id=1, source_target_pairs={{0,2},{1,3},{2,0},{3,1},{4,6},{5,7},{6,4},{7,5},{8,10},{9,11},{10,... | collective-permute-start | bytes 98312 | tf_op jit(solution)/shard_map/basis_pair/ppermute | solution.py:28
  25.8 3.0 %collective-permute-start.2 = (f32[16,512]{1,0:T(8,128)}, f32[16,512]{1,0:T(8,128)S(1)}, u32[]{:S(2)}, u32[]{:S(2)}) collective-permute-start(f32[16,512]{1,0:T(8,128)} %param.7), channel_id=1, source_target_pairs={{0,3},{1,0},{2,1},{3,2},{4,7},{5,4},{6,5},{7,6},{8,11},{9,8},{10,9... | collective-permute-start | bytes 98312 | tf_op jit(solution)/shard_map/basis_pair/ppermute | solution.py:28
  28.8 0.8 bitcast_dynamic-update-slice_fusion.7
  29.6 0.0 collective-permute-done
  29.6 0.0 collective-permute-done.1
  29.6 1.3 collective-permute-done.2
  30.9 4.3 %collective-permute-start.3 = (f32[4,16,512]{2,1,0:T(8,128)S(1)}, f32[4,16,512]{2,1,0:T(8,128)S(1)}, u32[]{:S(2)}, u32[]{:S(2)}) collective-permute-start(f32[4,16,512]{2,1,0:T(8,128)S(1)} %bitcast_dynamic-update-slice_fusion.4), channel_id=1, source_target_pairs={{0,64},{64,0},{1,65},{65,1},{2,66},{66,2},{3,67},{67,3},{4,68},{68... | collective-permute-start | bytes 393224 | tf_op jit(solution)/shard_map/basis_pair/ppermute | solution.py:28
  35.3 0.1 copy_dynamic-update-slice_fusion.1
  35.4 0.8 collective-permute-done.3
  36.2 0.1 copy_dynamic-update-slice_fusion
  36.3 4.6 %all-to-all-done = bf16[16,128,128]{2,1,0:T(8,128)(2,1)S(1)} async-done(((bf16[16,128,128]{2,1,0:T(8,128)(2,1)}), bf16[16,128,128]{2,1,0:T(8,128)(2,1)S(1)}, u32[]{:S(2)}, u32[]{:S(2)}) %all-to-all-start) | async-done | bytes 524320 | tf_op jit(solution)/shard_map/entries_z/all_to_all | solution.py:19
  40.8 1.8 %broadcast_in_dim.79 = bf16[4,16,128,128]{3,2,1,0:T(8,128)(2,1)} broadcast(bf16[16,128,128]{2,1,0:T(8,128)(2,1)S(1)} %all-to-all-done), dimensions={1,2,3} | broadcast | bytes 2621440 | tf_op jit(solution)/shard_map/entries_y/broadcast_in_dim | solution.py:18
  42.7 4.2 %all-to-all-start.1 = ((bf16[4,16,128,128]{3,2,1,0:T(8,128)(2,1)}), bf16[4,16,128,128]{3,2,1,0:T(8,128)(2,1)S(1)}, u32[]{:S(2)}, u32[]{:S(2)}) async-start(bf16[4,16,128,128]{3,2,1,0:T(8,128)(2,1)} %broadcast_in_dim.79), calls=%async_computation.1 | async-start | bytes 4194304 | tf_op jit(solution)/shard_map/entries_y/all_to_all | solution.py:19
  46.9 3.1 %collective-permute-start.4 = (f32[2,4,16,512]{3,1,2,0:T(4,128)S(1)}, f32[2,4,16,512]{3,1,2,0:T(4,128)}, u32[]{:S(2)}, u32[]{:S(2)}) collective-permute-start(f32[2,4,16,512]{3,1,2,0:T(4,128)S(1)} %copy_dynamic-update-slice_fusion), channel_id=1, source_target_pairs={{0,128},{128,256},{256,384},{384,0},{1,129},{129,257},{257,385},{3... | collective-permute-start | bytes 786440 | tf_op jit(solution)/shard_map/basis_plane/ppermute | solution.py:28
  50.0 4.4 %collective-permute-start.5 = (f32[2,4,16,512]{3,1,2,0:T(4,128)S(1)}, f32[2,4,16,512]{3,1,2,0:T(4,128)S(1)}, u32[]{:S(2)}, u32[]{:S(2)}) collective-permute-start(f32[2,4,16,512]{3,1,2,0:T(4,128)S(1)} %copy_dynamic-update-slice_fusion), channel_id=1, source_target_pairs={{0,256},{128,384},{256,0},{384,128},{1,257},{129,385},{257,1},{385... | collective-permute-start | bytes 786440 | tf_op jit(solution)/shard_map/basis_plane/ppermute | solution.py:28
  54.4 3.1 %collective-permute-start.6 = (f32[2,4,16,512]{3,1,2,0:T(4,128)S(1)}, f32[2,4,16,512]{3,1,2,0:T(4,128)S(1)}, u32[]{:S(2)}, u32[]{:S(2)}) collective-permute-start(f32[2,4,16,512]{3,1,2,0:T(4,128)S(1)} %copy_dynamic-update-slice_fusion), channel_id=1, source_target_pairs={{0,384},{128,0},{256,128},{384,256},{1,385},{129,1},{257,129},{385... | collective-permute-start | bytes 786440 | tf_op jit(solution)/shard_map/basis_plane/ppermute | solution.py:28
  57.5 0.2 broadcast_in_dim.80
  57.7 0.0 collective-permute-done.4
  57.7 1.0 bitcast_dynamic-update-slice_fusion.2
  58.7 0.3 collective-permute-done.5
  59.0 2.9 %collective-permute-done.6 = f32[2,4,16,512]{3,1,2,0:T(4,128)S(1)} collective-permute-done((f32[2,4,16,512]{3,1,2,0:T(4,128)S(1)}, f32[2,4,16,512]{3,1,2,0:T(4,128)S(1)}, u32[]{:S(2)}, u32[]{:S(2)}) %collective-permute-start.6) | collective-permute-done | bytes 262176 | tf_op jit(solution)/shard_map/basis_plane/ppermute | solution.py:28
  61.9 0.3 copy.22
  62.3 0.8 constant_dynamic-slice_fusion.1
  63.1 1.1 copy.23
  64.1 0.0 copy-start
  64.1 1.4 copy.24
  65.6 1.6 %reshape.39.basis = f32[512,512]{1,0:T(8,128)S(1)} reshape(f32[8,4,4,4,512]{4,3,2,1,0:T(4,128)} %copy.24) | data formatting | bytes 2097152 | tf_op jit(solution)/shard_map/basis_plane/reshape | solution.py:145
  67.1 0.0 all-to-all-done.1.entries
  67.1 0.0 copy-done
  67.2 3.8 %slab.1 = f32[32,12,128]{2,1,0:T(8,128)S(1)} custom-call(bf16[2,128,8192]{2,1,0:T(8,128)(2,1)} %impedance.1, f32[128,16]{1,0:T(8,128)S(1)} %bitcast.34, bf16[4,16,128,128]{3,2,1,0:T(8,128)(2,1)S(1)} %all-to-all-done.1.entries, f32[512,128]{1,0:T(8,128)S(1)} %bitcast.33), custom_call_target="tpu_custom_call" | custom-call | flops 536870912 | bytes 6291456 | tf_op jit(solution)/shard_map/slab/pallas_call | solution.py:76
  71.0 24.5 %all_to_all.34 = f32[32,12,128]{2,1,0:T(8,128)S(1)} all-to-all(f32[32,12,128]{2,1,0:T(8,128)S(1)} %slab.1), channel_id=1, replica_groups=mesh['x'=4,'core'=2,'z'=16,'y'=4] {'x','core','y'}, dimensions={0} | all-to-all | bytes 393216 | tf_op jit(solution)/shard_map/sums_plane/all_to_all | solution.py:152
  95.5 20.2 %all_to_all.35 = f32[16,8,128]{2,1,0:T(8,128)S(1)} all-to-all(f32[16,8,128]{2,1,0:T(8,128)S(1)} %broadcast_in_dim.86), channel_id=1, replica_groups=mesh['x'=4,'core'=2,'z'=16,'y'=4] {'z'}, dimensions={0} | all-to-all | bytes 131072 | tf_op jit(solution)/shard_map/coefficients_z/all_to_all | solution.py:19
  115.8 15.5 %all_to_all.36.taken = f32[32,24,128]{2,1,0:T(8,128)S(1)} all-to-all(f32[32,24,128]{2,1,0:T(8,128)S(1)} %broadcast_in_dim.87), channel_id=1, replica_groups=mesh['x'=4,'core'=2,'z'=16,'y'=4] {'x','core','y'}, dimensions={0} | all-to-all | bytes 786432 | tf_op jit(solution)/shard_map/gather_plane/all_to_all | solution.py:19
  131.4 1.1 residual.1
  132.5 13.8 %all_to_all.37 = f32[16,1,128]{2,1,0:T(1,128)S(1)} all-to-all(f32[16,1,128]{2,1,0:T(1,128)S(1)} %bitcast.35), channel_id=1, replica_groups=mesh['x'=4,'core'=2,'z'=16,'y'=4] {'z'}, dimensions={0} | all-to-all | bytes 16384 | tf_op jit(solution)/shard_map/squares/all_to_all | solution.py:169
  146.3 0.1 add_rsqrt_fusion
  146.4 0.1 pad_maximum_fusion.1
  146.5 0.6 broadcast_multiply_fusion
  (18 shorter events, 0.3 us)
Async XLA Ops:
  2.3 38.6 %all-to-all-start = ((bf16[16,128,128]{2,1,0:T(8,128)(2,1)}), bf16[16,128,128]{2,1,0:T(8,128)(2,1)S(1)}, u32[]{:S(2)}, u32[]{:S(2)}) async-start(bf16[16,128,128]{2,1,0:T(8,128)(2,1)} %broadcast_in_dim.70), calls=%async_computation | async-start | bytes 1048576 | tf_op jit(solution)/shard_map/entries_z/all_to_all | solution.py:19
  18.0 11.6 %collective-permute-start = (f32[16,512]{1,0:T(8,128)}, f32[16,512]{1,0:T(8,128)S(1)}, u32[]{:S(2)}, u32[]{:S(2)}) collective-permute-start(f32[16,512]{1,0:T(8,128)} %param.7), channel_id=1, source_target_pairs={{0,1},{1,2},{2,3},{3,0},{4,5},{5,6},{6,7},{7,4},{8,9},{9,10},{10,1... | collective-permute-start | bytes 98312 | tf_op jit(solution)/shard_map/basis_pair/ppermute | solution.py:28
  21.2 8.4 %collective-permute-start.1 = (f32[16,512]{1,0:T(8,128)}, f32[16,512]{1,0:T(8,128)S(1)}, u32[]{:S(2)}, u32[]{:S(2)}) collective-permute-start(f32[16,512]{1,0:T(8,128)} %param.7), channel_id=1, source_target_pairs={{0,2},{1,3},{2,0},{3,1},{4,6},{5,7},{6,4},{7,5},{8,10},{9,11},{10,... | collective-permute-start | bytes 98312 | tf_op jit(solution)/shard_map/basis_pair/ppermute | solution.py:28
  25.8 5.2 %collective-permute-start.2 = (f32[16,512]{1,0:T(8,128)}, f32[16,512]{1,0:T(8,128)S(1)}, u32[]{:S(2)}, u32[]{:S(2)}) collective-permute-start(f32[16,512]{1,0:T(8,128)} %param.7), channel_id=1, source_target_pairs={{0,3},{1,0},{2,1},{3,2},{4,7},{5,4},{6,5},{7,6},{8,11},{9,8},{10,9... | collective-permute-start | bytes 98312 | tf_op jit(solution)/shard_map/basis_pair/ppermute | solution.py:28
  30.9 5.2 %collective-permute-start.3 = (f32[4,16,512]{2,1,0:T(8,128)S(1)}, f32[4,16,512]{2,1,0:T(8,128)S(1)}, u32[]{:S(2)}, u32[]{:S(2)}) collective-permute-start(f32[4,16,512]{2,1,0:T(8,128)S(1)} %bitcast_dynamic-update-slice_fusion.4), channel_id=1, source_target_pairs={{0,64},{64,0},{1,65},{65,1},{2,66},{66,2},{3,67},{67,3},{4,68},{68... | collective-permute-start | bytes 393224 | tf_op jit(solution)/shard_map/basis_pair/ppermute | solution.py:28
  42.7 24.4 %all-to-all-start.1 = ((bf16[4,16,128,128]{3,2,1,0:T(8,128)(2,1)}), bf16[4,16,128,128]{3,2,1,0:T(8,128)(2,1)S(1)}, u32[]{:S(2)}, u32[]{:S(2)}) async-start(bf16[4,16,128,128]{3,2,1,0:T(8,128)(2,1)} %broadcast_in_dim.79), calls=%async_computation.1 | async-start | bytes 4194304 | tf_op jit(solution)/shard_map/entries_y/all_to_all | solution.py:19
  46.9 10.8 %collective-permute-start.4 = (f32[2,4,16,512]{3,1,2,0:T(4,128)S(1)}, f32[2,4,16,512]{3,1,2,0:T(4,128)}, u32[]{:S(2)}, u32[]{:S(2)}) collective-permute-start(f32[2,4,16,512]{3,1,2,0:T(4,128)S(1)} %copy_dynamic-update-slice_fusion), channel_id=1, source_target_pairs={{0,128},{128,256},{256,384},{384,0},{1,129},{129,257},{257,385},{3... | collective-permute-start | bytes 786440 | tf_op jit(solution)/shard_map/basis_plane/ppermute | solution.py:28
  50.0 9.0 %collective-permute-start.5 = (f32[2,4,16,512]{3,1,2,0:T(4,128)S(1)}, f32[2,4,16,512]{3,1,2,0:T(4,128)S(1)}, u32[]{:S(2)}, u32[]{:S(2)}) collective-permute-start(f32[2,4,16,512]{3,1,2,0:T(4,128)S(1)} %copy_dynamic-update-slice_fusion), channel_id=1, source_target_pairs={{0,256},{128,384},{256,0},{384,128},{1,257},{129,385},{257,1},{385... | collective-permute-start | bytes 786440 | tf_op jit(solution)/shard_map/basis_plane/ppermute | solution.py:28
  54.4 7.5 %collective-permute-start.6 = (f32[2,4,16,512]{3,1,2,0:T(4,128)S(1)}, f32[2,4,16,512]{3,1,2,0:T(4,128)S(1)}, u32[]{:S(2)}, u32[]{:S(2)}) collective-permute-start(f32[2,4,16,512]{3,1,2,0:T(4,128)S(1)} %copy_dynamic-update-slice_fusion), channel_id=1, source_target_pairs={{0,384},{128,0},{256,128},{384,256},{1,385},{129,1},{257,129},{385... | collective-permute-start | bytes 786440 | tf_op jit(solution)/shard_map/basis_plane/ppermute | solution.py:28
  64.1 3.0 %copy-start = (f32[8,16]{1,0:T(8,128)S(1)}, f32[8,16]{1,0:T(8,128)}, u32[]{:S(2)}) copy-start(f32[8,16]{1,0:T(8,128)} %param.5) | copy-start | bytes 1540

commit v3 on v2

--- a/solution.py
+++ b/solution.py
@@ -5,6 +5,7 @@
 from jax import lax
 from jax.experimental import pallas as pl
 from jax.experimental.pallas import tpu as pltpu
+from jax.experimental.layout import Layout, with_layout_constraint
 from jax.sharding import Mesh, PartitionSpec as P
 
 ROW = ("x", "core")
@@ -88,23 +89,28 @@
     )(impedance, scales, entries, basis)
 
 
-def residual_kernel(taken, basis, coefficients, residual, sums):
+def residual_kernel(taken, basis, coefficients, residual, sums, product):
     members, height, columns = taken.shape
+    rows, width = basis.shape
     count = coefficients.shape[0]
     half = columns // 2
-    found = taken[:, : count // members, :].reshape(count, columns)
-    product = taken[:, count // members :, :].reshape(residual.shape)
+    head = count // members
+    share = rows // members
+    for member in range(members):
+        product[member * share : (member + 1) * share] = taken[member, head:]
+    found = taken[:, :head, :].reshape(count, columns)
     coefficients[...] = found
     turned = turn(found, -1.0, 1.0)
     pair = [found.reshape(-1, 1, half, columns), turned.reshape(-1, 1, half, columns)]
-    both = jnp.concatenate(pair, 1).reshape(2 * count, columns)
-    rest = product - jnp.dot(basis[...], both, precision=HIGHEST, preferred_element_type=jnp.float32)
+    both = jnp.concatenate(pair, 1).reshape(width, columns)
+    known = jnp.dot(basis[...], both, precision=HIGHEST, preferred_element_type=jnp.float32)
+    rest = product[...] - known
     residual[...] = rest
     sums[...] = jnp.broadcast_to(jnp.sum(rest * rest, axis=0, keepdims=True), sums.shape)
 
 
-def plane_residual(taken, basis, copies):
-    members, height, columns = taken.shape
+def rows_residual(taken, basis, copies):
+    columns = taken.shape[2]
     rows, width = basis.shape
     vmem = pl.BlockSpec(memory_space=pltpu.VMEM)
     shapes = [(width // 2, columns), (rows, columns), (copies, columns)]
@@ -113,6 +119,7 @@
         out_shape=[jax.ShapeDtypeStruct(shape, jnp.float32) for shape in shapes],
         in_specs=[vmem, vmem],
         out_specs=[vmem] * 3,
+        scratch_shapes=[pltpu.VMEM((rows, columns), jnp.float32)],
         compiler_params=pltpu.CompilerParams(vmem_limit_bytes=24 * 2**20),
         cost_estimate=pl.CostEstimate(
             flops=12 * rows * width * columns,
@@ -128,45 +135,42 @@
     width = prior_basis.shape[1]
     own_rows = prior_basis.shape[0]
     rows = impedance.shape[1]
-    ys, zs, row_members, members = (lax.axis_size(axes) for axes in ("y", "z", ROW, PLANE))
+    ys, row_members, members = (lax.axis_size(axes) for axes in ("y", ROW, PLANE))
     share = rows // members
     height = width // 2 // members
-    with jax.named_scope("basis_pair"):
-        pair = ring_gather(ring_gather(prior_basis, "y"), "core")
     with jax.named_scope("entries_z"):
-        along_z = spread(krylov_block, "z")
+        along_z = lax.all_gather(krylov_block, "z", axis=0)
+        along_z, prior = lax.optimization_barrier((along_z, prior_basis))
     with jax.named_scope("entries_y"):
-        along_z, pair = lax.optimization_barrier((along_z, pair))
         entries = spread(along_z, "y")
-    with jax.named_scope("basis_plane"):
-        gathered = ring_gather(pair, "x").reshape(row_members, ys, own_rows, width)
-        here = lax.dynamic_index_in_dim(gathered, lax.axis_index("y"), 1, False).reshape(rows, width).T
-        basis = gathered.reshape(row_members, ys, own_rows // share, share, width)
-        basis = jnp.swapaxes(basis, 1, 2).reshape(members * ys * share, width)
-        row, y = lax.axis_index(ROW).astype(jnp.int32), lax.axis_index("y").astype(jnp.int32)
+    with jax.named_scope("basis_rows"):
+        here = ring_gather(ring_gather(prior, "core"), "x").reshape(rows, width)
+    with jax.named_scope("stage"):
         scales = jnp.repeat(tile_scale, rows // tile_scale.shape[0], axis=0)
-        entries, here, basis, scales, row, y = lax.optimization_barrier((entries, here, basis, scales, row, y))
+        start = (lax.axis_index(ROW) * own_rows).astype(jnp.int32)
+        turned = with_layout_constraint(here.T, Layout((0, 1)))
+        held = (entries, scales, here, turned, start)
+        entries, scales, here, turned, start = lax.optimization_barrier(held)
     with jax.named_scope("slab"):
-        parts = slab_sums(impedance, scales, entries, here, members)
+        parts = slab_sums(impedance, scales, entries, turned, members)
     with jax.named_scope("sums_plane"):
         taken = lax.all_to_all(parts, PLANE, 0, 0, tiled=True)
         chunk = jnp.sum(taken[:, :height], axis=0)
-        product = jnp.sum(taken[:, height:].reshape(row_members, ys * share, columns), axis=0)
+        product = jnp.sum(taken[:, height:].reshape(row_members, ys, share, columns), axis=0)
         chunk, product = lax.optimization_barrier((chunk, product))
     with jax.named_scope("coefficients_z"):
         chunk = jnp.sum(spread(chunk, "z"), axis=0)
     with jax.named_scope("gather_plane"):
-        taken = spread(jnp.concatenate([chunk, product], 0), PLANE)
+        parts = jnp.broadcast_to(product[None], (row_members,) + product.shape).reshape(members, share, columns)
+        parts = jnp.concatenate([jnp.broadcast_to(chunk[None], (members,) + chunk.shape), parts], 1)
+        taken = lax.all_to_all(parts, PLANE, 0, 0, tiled=True)
     with jax.named_scope("residual"):
-        coefficients, residual, sums = plane_residual(taken, basis, zs)
-        own = residual.reshape(row_members, own_rows // share, ys, share, columns)
-        sizes = (1, own_rows // share, 1, share, columns)
+        coefficients, residual, sums = rows_residual(taken, here, lax.axis_size(COL))
         zero = jnp.int32(0)
-        own = lax.dynamic_slice(own, (row, zero, y, zero, zero), sizes, allow_negative_indices=False)
-        own = own.reshape(own_rows, columns)
+        own = lax.dynamic_slice(residual, (start, zero), (own_rows, columns), allow_negative_indices=False)
         own, sums = lax.optimization_barrier((own, sums))
     with jax.named_scope("squares"):
-        sums = jnp.sum(lax.all_to_all(sums, "z", 0, 0, tiled=True), axis=0)
+        sums = jnp.sum(lax.all_to_all(sums, COL, 0, 0, tiled=True), axis=0)
         squares = sums[:half] + sums[half:]
     with jax.named_scope("scale"):
         total_rows = own_rows * lax.axis_size(ROW + COL)

time: 148 us -> 136 us (0.919)
  blocking collectives: 74 us -> 98.8 us
  starting transfers between devices: 45.4 us -> 25.3 us
  local copies, waits for them, and re-layouts: 11 us -> 2.13 us
  waiting for transfers between devices: 9.89 us -> 2.89 us
    all_gather x0 -> x1, blocking collectives: none -> 32.1 us  [per_device(): along_z = lax.all_gather(krylov_block, 'z', axis=0)]
    all_to_all x2 -> x1, blocking collectives: 35.8 us -> 17.7 us  [spread(): return lax.all_to_all(copies, axes, 0, 0, tiled=True)]
    all_to_all x2 -> x1, starting transfers between devices: 19.9 us -> 4.31 us  [spread(): return lax.all_to_all(copies, axes, 0, 0, tiled=True)]
    all_to_all x1 -> x2, blocking collectives: 24.5 us -> 31.7 us  [per_device(): taken = lax.all_to_all(parts, PLANE, 0, 0, tiled=True)]
    all_to_all x2 -> x1, waiting for transfers between devices: 4.57 us -> 0.01 us  [spread(): return lax.all_to_all(copies, axes, 0, 0, tiled=True)]
    ppermute x7 -> x4, starting transfers between devices: 25.5 us -> 20.9 us  [ring_gather(): arrived = lax.ppermute(block, axis, pairs) if step else block]
    all_to_all x1, blocking collectives: 13.8 us -> 17.3 us  [per_device(): sums = jnp.sum(lax.all_to_all(sums, COL, 0, 0, tiled=True), axis=0)]
    reshape x2 -> x0, local copies, waits for them, and re-layouts: 2.65 us -> none  [the longest x1 1.58 us: per_device(): basis = jnp.swapaxes(basis, 1, 2).reshape(members * ys * share, width)]
  transfers between devices with their start and end apart: 9 -> 5, of which waited for: 5 -> 2; matrix products, arithmetic and copies ran while one was open for 5% -> 0% of each run, Pallas kernels for 0% -> 0%
where the time goes in v3:
time: 136 us
  blocking collectives  98.8 us (73%)
  starting transfers between devices  25.3 us (19%)
  Pallas kernels  4.84 us (4%)
  waiting for transfers between devices  2.89 us (2%)
  local copies, waits for them, and re-layouts  2.13 us (2%)
    all_gather x1, blocking collectives, per_device(): along_z = lax.all_gather(krylov_block, 'z', axis=0)  32.1 us
    all_to_all x2, blocking collectives, per_device(): taken = lax.all_to_all(parts, PLANE, 0, 0, tiled=True)  31.7 us
    ppermute x4, starting transfers between devices, ring_gather(): arrived = lax.ppermute(block, axis, pairs) if step else block  20.9 us
    all_to_all x1, blocking collectives, spread(): return lax.all_to_all(copies, axes, 0, 0, tiled=True)  17.7 us
    all_to_all x1, blocking collectives, per_device(): sums = jnp.sum(lax.all_to_all(sums, COL, 0, 0, tiled=True), axis=0)  17.3 us
    all_to_all x1, starting transfers between devices, spread(): return lax.all_to_all(copies, axes, 0, 0, tiled=True)  4.31 us
    pallas_call x1, Pallas kernels, slab_sums(): pl.pallas_call(functools.partial(slab_kernel, chunks), out_shape=jax.Shap...  3.82 us
    ppermute x4, waiting for transfers between devices, ring_gather(): arrived = lax.ppermute(block, axis, pairs) if step else block  2.89 us
  transfers between devices with their start and end apart: 5, of which 2 were waited for; matrix products, arithmetic and copies ran while one was open for 0% of the time, Pallas kernels for 0%

profile of v3, /device:TPU:1, one launch (start us, length us, event | category | flops | bytes accessed | tf_op | source)
XLA Modules:
  0.0 135.7 jit_solution(2631428546963280938)
XLA Ops:
  0.6 32.1 %all-gather = bf16[2048,128]{1,0:T(8,128)(2,1)S(1)} all-gather(bf16[128,128]{1,0:T(8,128)(2,1)} %param.6), channel_id=2, replica_groups=mesh['x'=4,'core'=2,'z'=16,'y'=4] {'z'}, dimensions={0}, use_global_device_ids=true | all-gather | bytes 557056 | tf_op jit(solution)/shard_map/entries_z/all_gather | solution.py:142
  32.7 1.9 %broadcast_in_dim.54 = bf16[4,16,128,128]{3,2,1,0:T(8,128)(2,1)} broadcast(bf16[16,128,128]{2,1,0:T(8,128)(2,1)S(1)} %bitcast.26), dimensions={1,2,3} | broadcast | bytes 2621440 | tf_op jit(solution)/shard_map/entries_y/broadcast_in_dim | solution.py:19
  34.6 0.0 copy-start
  34.6 0.0 copy-start.1
  34.6 4.3 %all-to-all-start = ((bf16[4,16,128,128]{3,2,1,0:T(8,128)(2,1)}), bf16[4,16,128,128]{3,2,1,0:T(8,128)(2,1)S(1)}, u32[]{:S(2)}, u32[]{:S(2)}) async-start(bf16[4,16,128,128]{3,2,1,0:T(8,128)(2,1)} %broadcast_in_dim.54), calls=%async_computation | async-start | bytes 4194304 | tf_op jit(solution)/shard_map/entries_y/all_to_all | solution.py:20
  38.9 0.0 copy-done
  38.9 10.4 %collective-permute-start = (f32[16,512]{1,0:T(8,128)S(1)}, f32[16,512]{1,0:T(8,128)S(1)}, u32[]{:S(2)}, u32[]{:S(2)}) collective-permute-start(f32[16,512]{1,0:T(8,128)S(1)} %copy-done), channel_id=1, source_target_pairs={{0,64},{64,0},{1,65},{65,1},{2,66},{66,2},{3,67},{67,3},{4,68},{68... | collective-permute-start | bytes 98312 | tf_op jit(solution)/shard_map/basis_rows/ppermute | solution.py:29
  49.4 0.8 collective-permute-done
  50.2 3.1 %collective-permute-start.1 = (f32[2,16,512]{2,1,0:T(8,128)S(1)}, f32[2,16,512]{2,1,0:T(8,128)S(1)}, u32[]{:S(2)}, u32[]{:S(2)}) collective-permute-start(f32[2,16,512]{2,1,0:T(8,128)S(1)} %bitcast_dynamic-update-slice_fusion.4), channel_id=1, source_target_pairs={{0,128},{128,256},{256,384},{384,0},{1,129},{129,257},{257,385},{3... | collective-permute-start | bytes 196616 | tf_op jit(solution)/shard_map/basis_rows/ppermute | solution.py:29
  53.3 4.4 %collective-permute-start.2 = (f32[2,16,512]{2,1,0:T(8,128)S(1)}, f32[2,16,512]{2,1,0:T(8,128)S(1)}, u32[]{:S(2)}, u32[]{:S(2)}) collective-permute-start(f32[2,16,512]{2,1,0:T(8,128)S(1)} %bitcast_dynamic-update-slice_fusion.4), channel_id=1, source_target_pairs={{0,256},{128,384},{256,0},{384,128},{1,257},{129,385},{257,1},{385... | collective-permute-start | bytes 196616 | tf_op jit(solution)/shard_map/basis_rows/ppermute | solution.py:29
  57.6 3.1 %collective-permute-start.3 = (f32[2,16,512]{2,1,0:T(8,128)S(1)}, f32[2,16,512]{2,1,0:T(8,128)S(1)}, u32[]{:S(2)}, u32[]{:S(2)}) collective-permute-start(f32[2,16,512]{2,1,0:T(8,128)S(1)} %bitcast_dynamic-update-slice_fusion.4), channel_id=1, source_target_pairs={{0,384},{128,0},{256,128},{384,256},{1,385},{129,1},{257,129},{385... | collective-permute-start | bytes 196616 | tf_op jit(solution)/shard_map/basis_rows/ppermute | solution.py:29
  60.7 0.0 collective-permute-done.1
  60.8 0.0 collective-permute-done.2
  60.8 2.1 %collective-permute-done.3 = f32[2,16,512]{2,1,0:T(8,128)S(1)} collective-permute-done((f32[2,16,512]{2,1,0:T(8,128)S(1)}, f32[2,16,512]{2,1,0:T(8,128)S(1)}, u32[]{:S(2)}, u32[]{:S(2)}) %collective-permute-start.3) | collective-permute-done | bytes 65568 | tf_op jit(solution)/shard_map/basis_rows/ppermute | solution.py:29
  62.9 0.1 copy.9.basis
  63.1 0.0 all-to-all-done.entries
  63.1 0.0 copy-done.1
  63.1 3.8 %slab.1 = f32[32,12,128]{2,1,0:T(8,128)S(1)} custom-call(bf16[2,128,8192]{2,1,0:T(8,128)(2,1)} %impedance.1, f32[128,16]{1,0:T(8,128)S(1)} %bitcast.24, bf16[4,16,128,128]{3,2,1,0:T(8,128)(2,1)S(1)} %all-to-all-done.entries, f32[512,128]{1,0:T(8,128)S(1)} %copy.9.basis), custom_call_target="tpu_custom_call" | custom-call | flops 536870912 | bytes 6291456 | tf_op jit(solution)/shard_map/slab/pallas_call | solution.py:77
  66.9 17.4 %all_to_all.29 = f32[32,12,128]{2,1,0:T(8,128)S(1)} all-to-all(f32[32,12,128]{2,1,0:T(8,128)S(1)} %slab.1), channel_id=1, replica_groups=mesh['x'=4,'core'=2,'z'=16,'y'=4] {'x','core','y'}, dimensions={0} | all-to-all | bytes 393216 | tf_op jit(solution)/shard_map/sums_plane/all_to_all | solution.py:157
  84.4 17.7 %all_to_all.30 = f32[16,8,128]{2,1,0:T(8,128)S(1)} all-to-all(f32[16,8,128]{2,1,0:T(8,128)S(1)} %broadcast_in_dim.64), channel_id=1, replica_groups=mesh['x'=4,'core'=2,'z'=16,'y'=4] {'z'}, dimensions={0} | all-to-all | bytes 131072 | tf_op jit(solution)/shard_map/coefficients_z/all_to_all | solution.py:20
  102.2 14.3 %all_to_all.31.taken = f32[32,12,128]{2,1,0:T(8,128)S(1)} all-to-all(f32[32,12,128]{2,1,0:T(8,128)S(1)} %pad_maximum_fusion), channel_id=1, replica_groups=mesh['x'=4,'core'=2,'z'=16,'y'=4] {'x','core','y'}, dimensions={0} | all-to-all | bytes 393216 | tf_op jit(solution)/shard_map/gather_plane/all_to_all | solution.py:166
  116.5 1.0 residual.1
  117.6 17.3 %all_to_all.32 = f32[64,1,128]{2,1,0:T(1,128)S(1)} all-to-all(f32[64,1,128]{2,1,0:T(1,128)S(1)} %bitcast.25), channel_id=1, replica_groups=mesh['x'=4,'core'=2,'z'=16,'y'=4] {'z','y'}, dimensions={0} | all-to-all | bytes 65536 | tf_op jit(solution)/shard_map/squares/all_to_all | solution.py:173
  134.8 0.1 reduce_sum.39
  134.9 0.1 add_rsqrt_fusion
  135.0 0.1 pad_maximum_fusion.1
  135.1 0.6 broadcast_multiply_fusion
  (18 shorter events, 0.2 us)
Async XLA Ops:
  34.6 4.3 %copy-start = (f32[16,512]{1,0:T(8,128)S(1)}, f32[16,512]{1,0:T(8,128)}, u32[]{:S(2)}) copy-start(f32[16,512]{1,0:T(8,128)} %param.7) | copy-start | bytes 98308
  34.6 28.5 %copy-start.1 = (f32[8,16]{1,0:T(8,128)S(1)}, f32[8,16]{1,0:T(8,128)}, u32[]{:S(2)}) copy-start(f32[8,16]{1,0:T(8,128)} %param.5) | copy-start | bytes 1540
  34.6 28.5 %all-to-all-start = ((bf16[4,16,128,128]{3,2,1,0:T(8,128)(2,1)}), bf16[4,16,128,128]{3,2,1,0:T(8,128)(2,1)S(1)}, u32[]{:S(2)}, u32[]{:S(2)}) async-start(bf16[4,16,128,128]{3,2,1,0:T(8,128)(2,1)} %broadcast_in_dim.54), calls=%async_computation | async-start | bytes 4194304 | tf_op jit(solution)/shard_map/entries_y/all_to_all | solution.py:20
  38.9 11.3 %collective-permute-start = (f32[16,512]{1,0:T(8,128)S(1)}, f32[16,512]{1,0:T(8,128)S(1)}, u32[]{:S(2)}, u32[]{:S(2)}) collective-permute-start(f32[16,512]{1,0:T(8,128)S(1)} %copy-done), channel_id=1, source_target_pairs={{0,64},{64,0},{1,65},{65,1},{2,66},{66,2},{3,67},{67,3},{4,68},{68... | collective-permute-start | bytes 98312 | tf_op jit(solution)/shard_map/basis_rows/ppermute | solution.py:29
  50.2 10.6 %collective-permute-start.1 = (f32[2,16,512]{2,1,0:T(8,128)S(1)}, f32[2,16,512]{2,1,0:T(8,128)S(1)}, u32[]{:S(2)}, u32[]{:S(2)}) collective-permute-start(f32[2,16,512]{2,1,0:T(8,128)S(1)} %bitcast_dynamic-update-slice_fusion.4), channel_id=1, source_target_pairs={{0,128},{128,256},{256,384},{384,0},{1,129},{129,257},{257,385},{3... | collective-permute-start | bytes 196616 | tf_op jit(solution)/shard_map/basis_rows/ppermute | solution.py:29
  53.3 7.5 %collective-permute-start.2 = (f32[2,16,512]{2,1,0:T(8,128)S(1)}, f32[2,16,512]{2,1,0:T(8,128)S(1)}, u32[]{:S(2)}, u32[]{:S(2)}) collective-permute-start(f32[2,16,512]{2,1,0:T(8,128)S(1)} %bitcast_dynamic-update-slice_fusion.4), channel_id=1, source_target_pairs={{0,256},{128,384},{256,0},{384,128},{1,257},{129,385},{257,1},{385... | collective-permute-start | bytes 196616 | tf_op jit(solution)/shard_map/basis_rows/ppermute | solution.py:29
  57.6 5.3 %collective-permute-start.3 = (f32[2,16,512]{2,1,0:T(8,128)S(1)}, f32[2,16,512]{2,1,0:T(8,128)S(1)}, u32[]{:S(2)}, u32[]{:S(2)}) collective-permute-start(f32[2,16,512]{2,1,0:T(8,128)S(1)} %bitcast_dynamic-update-slice_fusion.4), channel_id=1, source_target_pairs={{0,384},{128,0},{256,128},{384,256},{1,385},{129,1},{257,129},{385... | collective-permute-start | bytes 196616 | tf_op jit(solution)/shard_map/basis_rows/ppermute | solution.py:29

commit v4 on v3

--- a/solution.py
+++ b/solution.py
@@ -36,6 +36,26 @@
     half = block.shape[1] // 2
     lanes = lax.broadcasted_iota(jnp.int32, block.shape, 1)
     return pltpu.roll(block, half, 1) * jnp.where(lanes < half, first, second)
+
+
+def copies_kernel(source, out, sems):
+    size = out.shape[0]
+    copies = [pltpu.make_async_copy(source, out.at[i], sems.at[i]) for i in range(size)]
+    for copy in copies:
+        copy.start()
+    for copy in copies:
+        copy.wait()
+
+
+def copies_of(block, size):
+    return pl.pallas_call(
+        copies_kernel,
+        out_shape=jax.ShapeDtypeStruct((size,) + block.shape, block.dtype),
+        in_specs=[pl.BlockSpec(memory_space=pltpu.VMEM)],
+        out_specs=pl.BlockSpec(memory_space=pltpu.HBM),
+        scratch_shapes=[pltpu.SemaphoreType.DMA((size,))],
+        compiler_params=pltpu.CompilerParams(vmem_limit_bytes=8 * 2**20),
+    )(block)
 
 
 def slab_kernel(chunks, impedance, scales, entries, basis, out, held, sems):
@@ -89,17 +109,16 @@
     )(impedance, scales, entries, basis)
 
 
-def residual_kernel(taken, basis, coefficients, residual, sums, product):
+def residual_kernel(taken, basis, residual, sums, product):
     members, height, columns = taken.shape
     rows, width = basis.shape
-    count = coefficients.shape[0]
+    count = width // 2
     half = columns // 2
     head = count // members
     share = rows // members
     for member in range(members):
         product[member * share : (member + 1) * share] = taken[member, head:]
     found = taken[:, :head, :].reshape(count, columns)
-    coefficients[...] = found
     turned = turn(found, -1.0, 1.0)
     pair = [found.reshape(-1, 1, half, columns), turned.reshape(-1, 1, half, columns)]
     both = jnp.concatenate(pair, 1).reshape(width, columns)
@@ -113,12 +132,12 @@
     columns = taken.shape[2]
     rows, width = basis.shape
     vmem = pl.BlockSpec(memory_space=pltpu.VMEM)
-    shapes = [(width // 2, columns), (rows, columns), (copies, columns)]
+    shapes = [(rows, columns), (copies, columns)]
     return pl.pallas_call(
         residual_kernel,
         out_shape=[jax.ShapeDtypeStruct(shape, jnp.float32) for shape in shapes],
         in_specs=[vmem, vmem],
-        out_specs=[vmem] * 3,
+        out_specs=[vmem] * 2,
         scratch_shapes=[pltpu.VMEM((rows, columns), jnp.float32)],
         compiler_params=pltpu.CompilerParams(vmem_limit_bytes=24 * 2**20),
         cost_estimate=pl.CostEstimate(
@@ -129,9 +148,29 @@
     )(taken, basis)
 
 
+def scale_kernel(total_rows, sums, own, taken, coefficients, new_basis):
+    count, columns = coefficients.shape
+    coefficients[...] = taken[:, : count // taken.shape[0], :].reshape(count, columns)
+    squares = sums[...] + turn(sums[...], 1.0, 1.0)
+    factor = 1.0 / jnp.sqrt(squares / total_rows + 1e-06)
+    new_basis[...] = own[...] * factor
+
+
+def scaled(sums, own, taken, count, total_rows):
+    columns = own.shape[1]
+    vmem = pl.BlockSpec(memory_space=pltpu.VMEM)
+    shapes = [(count, columns), own.shape]
+    return pl.pallas_call(
+        functools.partial(scale_kernel, total_rows),
+        out_shape=[jax.ShapeDtypeStruct(shape, jnp.float32) for shape in shapes],
+        in_specs=[vmem] * 3,
+        out_specs=[vmem] * 2,
+        compiler_params=pltpu.CompilerParams(vmem_limit_bytes=16 * 2**20),
+    )(sums, own, taken)
+
+
 def per_device(impedance, tile_scale, krylov_block, prior_basis):
     columns = krylov_block.shape[1]
-    half = columns // 2
     width = prior_basis.shape[1]
     own_rows = prior_basis.shape[0]
     rows = impedance.shape[1]
@@ -142,7 +181,7 @@
         along_z = lax.all_gather(krylov_block, "z", axis=0)
         along_z, prior = lax.optimization_barrier((along_z, prior_basis))
     with jax.named_scope("entries_y"):
-        entries = spread(along_z, "y")
+        entries = lax.all_to_all(copies_of(along_z, ys), "y", 0, 0, tiled=True)
     with jax.named_scope("basis_rows"):
         here = ring_gather(ring_gather(prior, "core"), "x").reshape(rows, width)
     with jax.named_scope("stage"):
@@ -165,17 +204,15 @@
         parts = jnp.concatenate([jnp.broadcast_to(chunk[None], (members,) + chunk.shape), parts], 1)
         taken = lax.all_to_all(parts, PLANE, 0, 0, tiled=True)
     with jax.named_scope("residual"):
-        coefficients, residual, sums = rows_residual(taken, here, lax.axis_size(COL))
+        residual, sums = rows_residual(taken, here, lax.axis_size(COL))
         zero = jnp.int32(0)
         own = lax.dynamic_slice(residual, (start, zero), (own_rows, columns), allow_negative_indices=False)
         own, sums = lax.optimization_barrier((own, sums))
     with jax.named_scope("squares"):
         sums = jnp.sum(lax.all_to_all(sums, COL, 0, 0, tiled=True), axis=0)
-        squares = sums[:half] + sums[half:]
     with jax.named_scope("scale"):
         total_rows = own_rows * lax.axis_size(ROW + COL)
-        factor = 1.0 / jnp.sqrt(squares / total_rows + 1e-06)
-        new_basis = own * jnp.concatenate([factor, factor])[None, :]
+        coefficients, new_basis = scaled(sums[None], own, taken, width // 2, total_rows)
     return (coefficients, new_basis)
 
 

time: 136 us -> 135 us (level)
  local copies, waits for them, and re-layouts: 2.13 us -> 0.28 us
  Pallas kernels: 4.84 us -> 6.34 us
    pallas_call x0 -> x2, Pallas kernels: none -> 2.08 us  [the longest x1 1.39 us: copies_of(): pl.pallas_call(copies_kernel, out_shape=jax.ShapeDtypeStruct((size,) + bl...]
    broadcast_in_dim x2 -> x1, local copies, waits for them, and re-layouts: 1.87 us -> 0.01 us  [spread(): copies = jnp.broadcast_to(block[None], (size,) + block.shape)]
where the time goes in v4:
time: 135 us; the launch traced here: 134 us
  blocking collectives  98.8 us (73%)
  starting transfers between devices  25.1 us (19%)
  Pallas kernels  6.34 us (5%)
  waiting for transfers between devices  2.89 us (2%)
    all_gather x1, blocking collectives, per_device(): along_z = lax.all_gather(krylov_block, 'z', axis=0)  32.1 us
    all_to_all x2, blocking collectives, per_device(): taken = lax.all_to_all(parts, PLANE, 0, 0, tiled=True)  31.7 us
    ppermute x4, starting transfers between devices, ring_gather(): arrived = lax.ppermute(block, axis, pairs) if step else block  20.9 us
    all_to_all x1, blocking collectives, spread(): return lax.all_to_all(copies, axes, 0, 0, tiled=True)  17.7 us
    all_to_all x1, blocking collectives, per_device(): sums = jnp.sum(lax.all_to_all(sums, COL, 0, 0, tiled=True), axis=0)  17.3 us
    all_to_all x1, starting transfers between devices, per_device(): entries = lax.all_to_all(copies_of(along_z, ys), 'y', 0, 0, tiled=True)  4.2 us
    pallas_call x1, Pallas kernels, slab_sums(): pl.pallas_call(functools.partial(slab_kernel, chunks), out_shape=jax.Shap...  3.82 us
    ppermute x4, waiting for transfers between devices, ring_gather(): arrived = lax.ppermute(block, axis, pairs) if step else block  2.89 us
  transfers between devices with their start and end apart: 5, of which 2 were waited for; matrix products, arithmetic and copies ran while one was open for 0% of the time, Pallas kernels for 0%

profile of v4, /device:TPU:1, one launch (start us, length us, event | category | flops | bytes accessed | tf_op | source)
XLA Modules:
  0.0 134.5 jit_solution(15965984186592149998)
XLA Ops:
  0.6 32.1 %all-gather = bf16[2048,128]{1,0:T(8,128)(2,1)S(1)} all-gather(bf16[128,128]{1,0:T(8,128)(2,1)} %param.6), channel_id=2, replica_groups=mesh['x'=4,'core'=2,'z'=16,'y'=4] {'z'}, dimensions={0}, use_global_device_ids=true | all-gather | bytes 557056 | tf_op jit(solution)/shard_map/entries_z/all_gather | solution.py:181
  32.7 1.4 %entries_y.1 = bf16[4,16,128,128]{3,2,1,0:T(8,128)(2,1)} custom-call(bf16[16,128,128]{2,1,0:T(8,128)(2,1)S(1)} %bitcast.25), custom_call_target="tpu_custom_call" | custom-call | tf_op jit(solution)/shard_map/entries_y/pallas_call | solution.py:51
  34.1 0.0 copy-start
  34.1 0.0 copy-start.1
  34.1 4.2 %all-to-all-start = ((bf16[4,16,128,128]{3,2,1,0:T(8,128)(2,1)}), bf16[4,16,128,128]{3,2,1,0:T(8,128)(2,1)S(1)}, u32[]{:S(2)}, u32[]{:S(2)}) async-start(bf16[4,16,128,128]{3,2,1,0:T(8,128)(2,1)} %entries_y.1), calls=%async_computation | async-start | bytes 4194304 | tf_op jit(solution)/shard_map/entries_y/all_to_all | solution.py:184
  38.3 0.0 copy-done
  38.3 10.4 %collective-permute-start = (f32[16,512]{1,0:T(8,128)S(1)}, f32[16,512]{1,0:T(8,128)S(1)}, u32[]{:S(2)}, u32[]{:S(2)}) collective-permute-start(f32[16,512]{1,0:T(8,128)S(1)} %copy-done), channel_id=1, source_target_pairs={{0,64},{64,0},{1,65},{65,1},{2,66},{66,2},{3,67},{67,3},{4,68},{68... | collective-permute-start | bytes 98312 | tf_op jit(solution)/shard_map/basis_rows/ppermute | solution.py:29
  48.8 0.8 collective-permute-done
  49.6 3.1 %collective-permute-start.1 = (f32[2,16,512]{2,1,0:T(8,128)S(1)}, f32[2,16,512]{2,1,0:T(8,128)S(1)}, u32[]{:S(2)}, u32[]{:S(2)}) collective-permute-start(f32[2,16,512]{2,1,0:T(8,128)S(1)} %bitcast_dynamic-update-slice_fusion.4), channel_id=1, source_target_pairs={{0,128},{128,256},{256,384},{384,0},{1,129},{129,257},{257,385},{3... | collective-permute-start | bytes 196616 | tf_op jit(solution)/shard_map/basis_rows/ppermute | solution.py:29
  52.7 4.4 %collective-permute-start.2 = (f32[2,16,512]{2,1,0:T(8,128)S(1)}, f32[2,16,512]{2,1,0:T(8,128)S(1)}, u32[]{:S(2)}, u32[]{:S(2)}) collective-permute-start(f32[2,16,512]{2,1,0:T(8,128)S(1)} %bitcast_dynamic-update-slice_fusion.4), channel_id=1, source_target_pairs={{0,256},{128,384},{256,0},{384,128},{1,257},{129,385},{257,1},{385... | collective-permute-start | bytes 196616 | tf_op jit(solution)/shard_map/basis_rows/ppermute | solution.py:29
  57.1 3.1 %collective-permute-start.3 = (f32[2,16,512]{2,1,0:T(8,128)S(1)}, f32[2,16,512]{2,1,0:T(8,128)S(1)}, u32[]{:S(2)}, u32[]{:S(2)}) collective-permute-start(f32[2,16,512]{2,1,0:T(8,128)S(1)} %bitcast_dynamic-update-slice_fusion.4), channel_id=1, source_target_pairs={{0,384},{128,0},{256,128},{384,256},{1,385},{129,1},{257,129},{385... | collective-permute-start | bytes 196616 | tf_op jit(solution)/shard_map/basis_rows/ppermute | solution.py:29
  60.2 0.0 collective-permute-done.1
  60.2 0.0 collective-permute-done.2
  60.2 2.1 %collective-permute-done.3 = f32[2,16,512]{2,1,0:T(8,128)S(1)} collective-permute-done((f32[2,16,512]{2,1,0:T(8,128)S(1)}, f32[2,16,512]{2,1,0:T(8,128)S(1)}, u32[]{:S(2)}, u32[]{:S(2)}) %collective-permute-start.3) | collective-permute-done | bytes 65568 | tf_op jit(solution)/shard_map/basis_rows/ppermute | solution.py:29
  62.4 0.1 copy.9.basis
  62.5 0.0 all-to-all-done.entries
  62.5 0.0 copy-done.1
  62.5 3.8 %slab.1 = f32[32,12,128]{2,1,0:T(8,128)S(1)} custom-call(bf16[2,128,8192]{2,1,0:T(8,128)(2,1)} %impedance.1, f32[128,16]{1,0:T(8,128)S(1)} %bitcast.26, bf16[4,16,128,128]{3,2,1,0:T(8,128)(2,1)S(1)} %all-to-all-done.entries, f32[512,128]{1,0:T(8,128)S(1)} %copy.9.basis), custom_call_target="tpu_custom_call" | custom-call | flops 536870912 | bytes 6291456 | tf_op jit(solution)/shard_map/slab/pallas_call | solution.py:97
  66.4 17.4 %all_to_all.29 = f32[32,12,128]{2,1,0:T(8,128)S(1)} all-to-all(f32[32,12,128]{2,1,0:T(8,128)S(1)} %slab.1), channel_id=1, replica_groups=mesh['x'=4,'core'=2,'z'=16,'y'=4] {'x','core','y'}, dimensions={0} | all-to-all | bytes 393216 | tf_op jit(solution)/shard_map/sums_plane/all_to_all | solution.py:196
  83.9 17.7 %all_to_all.30 = f32[16,8,128]{2,1,0:T(8,128)S(1)} all-to-all(f32[16,8,128]{2,1,0:T(8,128)S(1)} %broadcast_in_dim.59), channel_id=1, replica_groups=mesh['x'=4,'core'=2,'z'=16,'y'=4] {'z'}, dimensions={0} | all-to-all | bytes 131072 | tf_op jit(solution)/shard_map/coefficients_z/all_to_all | solution.py:20
  101.6 14.3 %all_to_all.31.taken = f32[32,12,128]{2,1,0:T(8,128)S(1)} all-to-all(f32[32,12,128]{2,1,0:T(8,128)S(1)} %pad_maximum_fusion), channel_id=1, replica_groups=mesh['x'=4,'core'=2,'z'=16,'y'=4] {'x','core','y'}, dimensions={0} | all-to-all | bytes 393216 | tf_op jit(solution)/shard_map/gather_plane/all_to_all | solution.py:205
  116.0 0.4 residual.1
  116.4 17.3 %all_to_all.32 = f32[64,1,128]{2,1,0:T(1,128)S(1)} all-to-all(f32[64,1,128]{2,1,0:T(1,128)S(1)} %bitcast.27), channel_id=1, replica_groups=mesh['x'=4,'core'=2,'z'=16,'y'=4] {'z','y'}, dimensions={0} | all-to-all | bytes 65536 | tf_op jit(solution)/shard_map/squares/all_to_all | solution.py:212
  133.7 0.1 reduce_sum.39
  133.8 0.7 scale.1
  (18 shorter events, 0.2 us)
Async XLA Ops:
  34.1 4.2 %copy-start = (f32[16,512]{1,0:T(8,128)S(1)}, f32[16,512]{1,0:T(8,128)}, u32[]{:S(2)}) copy-start(f32[16,512]{1,0:T(8,128)} %param.7) | copy-start | bytes 98308
  34.1 28.4 %copy-start.1 = (f32[8,16]{1,0:T(8,128)S(1)}, f32[8,16]{1,0:T(8,128)}, u32[]{:S(2)}) copy-start(f32[8,16]{1,0:T(8,128)} %param.5) | copy-start | bytes 1540
  34.1 28.4 %all-to-all-start = ((bf16[4,16,128,128]{3,2,1,0:T(8,128)(2,1)}), bf16[4,16,128,128]{3,2,1,0:T(8,128)(2,1)S(1)}, u32[]{:S(2)}, u32[]{:S(2)}) async-start(bf16[4,16,128,128]{3,2,1,0:T(8,128)(2,1)} %entries_y.1), calls=%async_computation | async-start | bytes 4194304 | tf_op jit(solution)/shard_map/entries_y/all_to_all | solution.py:184
  38.3 11.3 %collective-permute-start = (f32[16,512]{1,0:T(8,128)S(1)}, f32[16,512]{1,0:T(8,128)S(1)}, u32[]{:S(2)}, u32[]{:S(2)}) collective-permute-start(f32[16,512]{1,0:T(8,128)S(1)} %copy-done), channel_id=1, source_target_pairs={{0,64},{64,0},{1,65},{65,1},{2,66},{66,2},{3,67},{67,3},{4,68},{68... | collective-permute-start | bytes 98312 | tf_op jit(solution)/shard_map/basis_rows/ppermute | solution.py:29
  49.6 10.6 %collective-permute-start.1 = (f32[2,16,512]{2,1,0:T(8,128)S(1)}, f32[2,16,512]{2,1,0:T(8,128)S(1)}, u32[]{:S(2)}, u32[]{:S(2)}) collective-permute-start(f32[2,16,512]{2,1,0:T(8,128)S(1)} %bitcast_dynamic-update-slice_fusion.4), channel_id=1, source_target_pairs={{0,128},{128,256},{256,384},{384,0},{1,129},{129,257},{257,385},{3... | collective-permute-start | bytes 196616 | tf_op jit(solution)/shard_map/basis_rows/ppermute | solution.py:29
  52.7 7.5 %collective-permute-start.2 = (f32[2,16,512]{2,1,0:T(8,128)S(1)}, f32[2,16,512]{2,1,0:T(8,128)S(1)}, u32[]{:S(2)}, u32[]{:S(2)}) collective-permute-start(f32[2,16,512]{2,1,0:T(8,128)S(1)} %bitcast_dynamic-update-slice_fusion.4), channel_id=1, source_target_pairs={{0,256},{128,384},{256,0},{384,128},{1,257},{129,385},{257,1},{385... | collective-permute-start | bytes 196616 | tf_op jit(solution)/shard_map/basis_rows/ppermute | solution.py:29
  57.1 5.3 %collective-permute-start.3 = (f32[2,16,512]{2,1,0:T(8,128)S(1)}, f32[2,16,512]{2,1,0:T(8,128)S(1)}, u32[]{:S(2)}, u32[]{:S(2)}) collective-permute-start(f32[2,16,512]{2,1,0:T(8,128)S(1)} %bitcast_dynamic-update-slice_fusion.4), channel_id=1, source_target_pairs={{0,384},{128,0},{256,128},{384,256},{1,385},{129,1},{257,129},{385... | collective-permute-start | bytes 196616 | tf_op jit(solution)/shard_map/basis_rows/ppermute | solution.py:29

commit v5 on v4

--- a/solution.py
+++ b/solution.py
@@ -62,8 +62,7 @@
     rows, columns = scales.shape[0], entries.shape[3]
     ys, zs, depth, _ = entries.shape
     width = ys * depth
-    members, height, _ = out.shape
-    share = rows // members
+    members, share, _ = out.shape
     span = zs * width // chunks
     copies = []
     for chunk in range(chunks):
@@ -83,20 +82,24 @@
     half = columns // 2
     inner = inner.reshape(-1, 2, half, columns)
     sums = inner[:, 0].reshape(-1, columns) + turn(inner[:, 1].reshape(-1, columns), 1.0, -1.0)
-    out[:, : height - share, :] = sums.reshape(members, height - share, columns)
+    step = sums.shape[0] // members
     for member in range(members):
-        out[member, height - share :, :] = partial[member * share : (member + 1) * share]
+        for first in range(0, step, share):
+            lanes = slice(first // share * columns, (first // share + 1) * columns)
+            out[member, :, lanes] = sums[member * step + first : member * step + first + share]
+        out[member, :, step // share * columns :] = partial[member * share : (member + 1) * share]
 
 
 def slab_sums(impedance, scales, entries, basis, members):
     rows = impedance.shape[1]
     columns = entries.shape[3]
     chunks = 4
-    height = (basis.shape[0] // 2 + rows) // members
+    share = rows // members
+    lanes = (basis.shape[0] // 2 // rows + 1) * columns
     vmem = pl.BlockSpec(memory_space=pltpu.VMEM)
     return pl.pallas_call(
         functools.partial(slab_kernel, chunks),
-        out_shape=jax.ShapeDtypeStruct((members, height, columns), jnp.float32),
+        out_shape=jax.ShapeDtypeStruct((members, share, lanes), jnp.float32),
         in_specs=[pl.BlockSpec(memory_space=pltpu.HBM), vmem, vmem, vmem],
         out_specs=vmem,
         scratch_shapes=[pltpu.VMEM(impedance.shape, impedance.dtype), pltpu.SemaphoreType.DMA((chunks,))],
@@ -109,18 +112,26 @@
     )(impedance, scales, entries, basis)
 
 
-def residual_kernel(taken, basis, residual, sums, product):
-    members, height, columns = taken.shape
+def unpack(taken, found):
+    members, share, _ = taken.shape
+    columns = found.shape[1]
+    step = found.shape[0] // members
+    for member in range(members):
+        for first in range(0, step, share):
+            lanes = slice(first // share * columns, (first // share + 1) * columns)
+            found[member * step + first : member * step + first + share] = taken[member, :, lanes]
+
+
+def residual_kernel(taken, basis, residual, sums, product, found):
+    members, share, _ = taken.shape
     rows, width = basis.shape
-    count = width // 2
+    count, columns = found.shape
     half = columns // 2
-    head = count // members
-    share = rows // members
     for member in range(members):
-        product[member * share : (member + 1) * share] = taken[member, head:]
-    found = taken[:, :head, :].reshape(count, columns)
-    turned = turn(found, -1.0, 1.0)
-    pair = [found.reshape(-1, 1, half, columns), turned.reshape(-1, 1, half, columns)]
+        product[member * share : (member + 1) * share] = taken[member, :, count // rows * columns :]
+    unpack(taken, found)
+    turned = turn(found[...], -1.0, 1.0)
+    pair = [found[...].reshape(-1, 1, half, columns), turned.reshape(-1, 1, half, columns)]
     both = jnp.concatenate(pair, 1).reshape(width, columns)
     known = jnp.dot(basis[...], both, precision=HIGHEST, preferred_element_type=jnp.float32)
     rest = product[...] - known
@@ -129,8 +140,8 @@
 
 
 def rows_residual(taken, basis, copies):
-    columns = taken.shape[2]
     rows, width = basis.shape
+    columns = taken.shape[2] // (width // 2 // rows + 1)
     vmem = pl.BlockSpec(memory_space=pltpu.VMEM)
     shapes = [(rows, columns), (copies, columns)]
     return pl.pallas_call(
@@ -138,7 +149,7 @@
         out_shape=[jax.ShapeDtypeStruct(shape, jnp.float32) for shape in shapes],
         in_specs=[vmem, vmem],
         out_specs=[vmem] * 2,
-        scratch_shapes=[pltpu.VMEM((rows, columns), jnp.float32)],
+        scratch_shapes=[pltpu.VMEM((count, columns), jnp.float32) for count in (rows, width // 2)],
         compiler_params=pltpu.CompilerParams(vmem_limit_bytes=24 * 2**20),
         cost_estimate=pl.CostEstimate(
             flops=12 * rows * width * columns,
@@ -149,8 +160,7 @@
 
 
 def scale_kernel(total_rows, sums, own, taken, coefficients, new_basis):
-    count, columns = coefficients.shape
-    coefficients[...] = taken[:, : count // taken.shape[0], :].reshape(count, columns)
+    unpack(taken, coefficients)
     squares = sums[...] + turn(sums[...], 1.0, 1.0)
     factor = 1.0 / jnp.sqrt(squares / total_rows + 1e-06)
     new_basis[...] = own[...] * factor
@@ -176,7 +186,7 @@
     rows = impedance.shape[1]
     ys, row_members, members = (lax.axis_size(axes) for axes in ("y", ROW, PLANE))
     share = rows // members
-    height = width // 2 // members
+    lanes = width // 2 // rows * columns
     with jax.named_scope("entries_z"):
         along_z = lax.all_gather(krylov_block, "z", axis=0)
         along_z, prior = lax.optimization_barrier((along_z, prior_basis))
@@ -194,14 +204,14 @@
         parts = slab_sums(impedance, scales, entries, turned, members)
     with jax.named_scope("sums_plane"):
         taken = lax.all_to_all(parts, PLANE, 0, 0, tiled=True)
-        chunk = jnp.sum(taken[:, :height], axis=0)
-        product = jnp.sum(taken[:, height:].reshape(row_members, ys, share, columns), axis=0)
+        chunk = jnp.sum(taken[:, :, :lanes], axis=0)
+        product = jnp.sum(taken[:, :, lanes:].reshape(row_members, ys, share, columns), axis=0)
         chunk, product = lax.optimization_barrier((chunk, product))
     with jax.named_scope("coefficients_z"):
         chunk = jnp.sum(spread(chunk, "z"), axis=0)
     with jax.named_scope("gather_plane"):
         parts = jnp.broadcast_to(product[None], (row_members,) + product.shape).reshape(members, share, columns)
-        parts = jnp.concatenate([jnp.broadcast_to(chunk[None], (members,) + chunk.shape), parts], 1)
+        parts = jnp.concatenate([jnp.broadcast_to(chunk[None], (members,) + chunk.shape), parts], 2)
         taken = lax.all_to_all(parts, PLANE, 0, 0, tiled=True)
     with jax.named_scope("residual"):
         residual, sums = rows_residual(taken, here, lax.axis_size(COL))

time: 135 us -> 134 us (level)
  blocking collectives: 98.8 us -> 97.4 us
where the time goes in v5:
time: 134 us; the launch traced here: 133 us
  blocking collectives  97.4 us (73%)
  starting transfers between devices  25.1 us (19%)
  Pallas kernels  6.35 us (5%)
  waiting for transfers between devices  2.89 us (2%)
    all_gather x1, blocking collectives, per_device(): along_z = lax.all_gather(krylov_block, 'z', axis=0)  32.1 us
    all_to_all x2, blocking collectives, per_device(): taken = lax.all_to_all(parts, PLANE, 0, 0, tiled=True)  30.4 us
    ppermute x4, starting transfers between devices, ring_gather(): arrived = lax.ppermute(block, axis, pairs) if step else block  20.9 us
    all_to_all x1, blocking collectives, spread(): return lax.all_to_all(copies, axes, 0, 0, tiled=True)  17.7 us
    all_to_all x1, blocking collectives, per_device(): sums = jnp.sum(lax.all_to_all(sums, COL, 0, 0, tiled=True), axis=0)  17.3 us
    all_to_all x1, starting transfers between devices, per_device(): entries = lax.all_to_all(copies_of(along_z, ys), 'y', 0, 0, tiled=True)  4.2 us
    pallas_call x1, Pallas kernels, slab_sums(): pl.pallas_call(functools.partial(slab_kernel, chunks), out_shape=jax.Shap...  3.82 us
    ppermute x4, waiting for transfers between devices, ring_gather(): arrived = lax.ppermute(block, axis, pairs) if step else block  2.89 us
  transfers between devices with their start and end apart: 5, of which 2 were waited for; matrix products, arithmetic and copies ran while one was open for 0% of the time, Pallas kernels for 0%

profile of v5, /device:TPU:1, one launch (start us, length us, event | category | flops | bytes accessed | tf_op | source)
XLA Modules:
  0.0 133.2 jit_solution(5873512977499692995)
XLA Ops:
  0.6 32.1 %all-gather = bf16[2048,128]{1,0:T(8,128)(2,1)S(1)} all-gather(bf16[128,128]{1,0:T(8,128)(2,1)} %param.6), channel_id=2, replica_groups=mesh['x'=4,'core'=2,'z'=16,'y'=4] {'z'}, dimensions={0}, use_global_device_ids=true | all-gather | bytes 557056 | tf_op jit(solution)/shard_map/entries_z/all_gather | solution.py:191
  32.7 1.4 %entries_y.1 = bf16[4,16,128,128]{3,2,1,0:T(8,128)(2,1)} custom-call(bf16[16,128,128]{2,1,0:T(8,128)(2,1)S(1)} %bitcast.25), custom_call_target="tpu_custom_call" | custom-call | tf_op jit(solution)/shard_map/entries_y/pallas_call | solution.py:51
  34.1 0.0 copy-start
  34.1 0.0 copy-start.1
  34.1 4.2 %all-to-all-start = ((bf16[4,16,128,128]{3,2,1,0:T(8,128)(2,1)}), bf16[4,16,128,128]{3,2,1,0:T(8,128)(2,1)S(1)}, u32[]{:S(2)}, u32[]{:S(2)}) async-start(bf16[4,16,128,128]{3,2,1,0:T(8,128)(2,1)} %entries_y.1), calls=%async_computation | async-start | bytes 4194304 | tf_op jit(solution)/shard_map/entries_y/all_to_all | solution.py:194
  38.3 0.0 copy-done
  38.3 10.4 %collective-permute-start = (f32[16,512]{1,0:T(8,128)S(1)}, f32[16,512]{1,0:T(8,128)S(1)}, u32[]{:S(2)}, u32[]{:S(2)}) collective-permute-start(f32[16,512]{1,0:T(8,128)S(1)} %copy-done), channel_id=1, source_target_pairs={{0,64},{64,0},{1,65},{65,1},{2,66},{66,2},{3,67},{67,3},{4,68},{68... | collective-permute-start | bytes 98312 | tf_op jit(solution)/shard_map/basis_rows/ppermute | solution.py:29
  48.8 0.8 collective-permute-done
  49.6 3.1 %collective-permute-start.1 = (f32[2,16,512]{2,1,0:T(8,128)S(1)}, f32[2,16,512]{2,1,0:T(8,128)S(1)}, u32[]{:S(2)}, u32[]{:S(2)}) collective-permute-start(f32[2,16,512]{2,1,0:T(8,128)S(1)} %bitcast_dynamic-update-slice_fusion.4), channel_id=1, source_target_pairs={{0,128},{128,256},{256,384},{384,0},{1,129},{129,257},{257,385},{3... | collective-permute-start | bytes 196616 | tf_op jit(solution)/shard_map/basis_rows/ppermute | solution.py:29
  52.7 4.4 %collective-permute-start.2 = (f32[2,16,512]{2,1,0:T(8,128)S(1)}, f32[2,16,512]{2,1,0:T(8,128)S(1)}, u32[]{:S(2)}, u32[]{:S(2)}) collective-permute-start(f32[2,16,512]{2,1,0:T(8,128)S(1)} %bitcast_dynamic-update-slice_fusion.4), channel_id=1, source_target_pairs={{0,256},{128,384},{256,0},{384,128},{1,257},{129,385},{257,1},{385... | collective-permute-start | bytes 196616 | tf_op jit(solution)/shard_map/basis_rows/ppermute | solution.py:29
  57.1 3.1 %collective-permute-start.3 = (f32[2,16,512]{2,1,0:T(8,128)S(1)}, f32[2,16,512]{2,1,0:T(8,128)S(1)}, u32[]{:S(2)}, u32[]{:S(2)}) collective-permute-start(f32[2,16,512]{2,1,0:T(8,128)S(1)} %bitcast_dynamic-update-slice_fusion.4), channel_id=1, source_target_pairs={{0,384},{128,0},{256,128},{384,256},{1,385},{129,1},{257,129},{385... | collective-permute-start | bytes 196616 | tf_op jit(solution)/shard_map/basis_rows/ppermute | solution.py:29
  60.2 0.0 collective-permute-done.1
  60.2 0.0 collective-permute-done.2
  60.2 2.1 %collective-permute-done.3 = f32[2,16,512]{2,1,0:T(8,128)S(1)} collective-permute-done((f32[2,16,512]{2,1,0:T(8,128)S(1)}, f32[2,16,512]{2,1,0:T(8,128)S(1)}, u32[]{:S(2)}, u32[]{:S(2)}) %collective-permute-start.3) | collective-permute-done | bytes 65568 | tf_op jit(solution)/shard_map/basis_rows/ppermute | solution.py:29
  62.4 0.1 copy.11.basis
  62.5 0.0 all-to-all-done.entries
  62.5 0.0 copy-done.1
  62.5 3.8 %slab.1 = f32[32,4,384]{2,1,0:T(4,128)S(1)} custom-call(bf16[2,128,8192]{2,1,0:T(8,128)(2,1)} %impedance.1, f32[128,16]{1,0:T(8,128)S(1)} %bitcast.26, bf16[4,16,128,128]{3,2,1,0:T(8,128)(2,1)S(1)} %all-to-all-done.entries, f32[512,128]{1,0:T(8,128)S(1)} %copy.11.basis), custom_call_target="tpu_custom_call" | custom-call | flops 536870912 | bytes 6291456 | tf_op jit(solution)/shard_map/slab/pallas_call | solution.py:100
  66.4 16.8 %all_to_all.29 = f32[32,4,384]{2,1,0:T(4,128)S(1)} all-to-all(f32[32,4,384]{2,1,0:T(4,128)S(1)} %slab.1), channel_id=1, replica_groups=mesh['x'=4,'core'=2,'z'=16,'y'=4] {'x','core','y'}, dimensions={0} | all-to-all | bytes 393216 | tf_op jit(solution)/shard_map/sums_plane/all_to_all | solution.py:206
  83.3 17.7 %all_to_all.30 = f32[16,4,256]{2,1,0:T(4,128)S(1)} all-to-all(f32[16,4,256]{2,1,0:T(4,128)S(1)} %broadcast_in_dim.59), channel_id=1, replica_groups=mesh['x'=4,'core'=2,'z'=16,'y'=4] {'z'}, dimensions={0} | all-to-all | bytes 131072 | tf_op jit(solution)/shard_map/coefficients_z/all_to_all | solution.py:20
  101.1 13.6 %all_to_all.31.taken = f32[32,4,384]{2,1,0:T(4,128)S(1)} all-to-all(f32[32,4,384]{2,1,0:T(4,128)S(1)} %pad_maximum_fusion), channel_id=1, replica_groups=mesh['x'=4,'core'=2,'z'=16,'y'=4] {'x','core','y'}, dimensions={0} | all-to-all | bytes 393216 | tf_op jit(solution)/shard_map/gather_plane/all_to_all | solution.py:215
  114.7 0.5 residual.1
  115.2 17.3 %all_to_all.32 = f32[64,1,128]{2,1,0:T(1,128)S(1)} all-to-all(f32[64,1,128]{2,1,0:T(1,128)S(1)} %bitcast.27), channel_id=1, replica_groups=mesh['x'=4,'core'=2,'z'=16,'y'=4] {'z','y'}, dimensions={0} | all-to-all | bytes 65536 | tf_op jit(solution)/shard_map/squares/all_to_all | solution.py:222
  132.5 0.1 reduce_sum.39
  132.5 0.7 scale.1
  (18 shorter events, 0.3 us)
Async XLA Ops:
  34.1 4.2 %copy-start = (f32[16,512]{1,0:T(8,128)S(1)}, f32[16,512]{1,0:T(8,128)}, u32[]{:S(2)}) copy-start(f32[16,512]{1,0:T(8,128)} %param.7) | copy-start | bytes 98308
  34.1 28.4 %copy-start.1 = (f32[8,16]{1,0:T(8,128)S(1)}, f32[8,16]{1,0:T(8,128)}, u32[]{:S(2)}) copy-start(f32[8,16]{1,0:T(8,128)} %param.5) | copy-start | bytes 1540
  34.1 28.4 %all-to-all-start = ((bf16[4,16,128,128]{3,2,1,0:T(8,128)(2,1)}), bf16[4,16,128,128]{3,2,1,0:T(8,128)(2,1)S(1)}, u32[]{:S(2)}, u32[]{:S(2)}) async-start(bf16[4,16,128,128]{3,2,1,0:T(8,128)(2,1)} %entries_y.1), calls=%async_computation | async-start | bytes 4194304 | tf_op jit(solution)/shard_map/entries_y/all_to_all | solution.py:194
  38.3 11.3 %collective-permute-start = (f32[16,512]{1,0:T(8,128)S(1)}, f32[16,512]{1,0:T(8,128)S(1)}, u32[]{:S(2)}, u32[]{:S(2)}) collective-permute-start(f32[16,512]{1,0:T(8,128)S(1)} %copy-done), channel_id=1, source_target_pairs={{0,64},{64,0},{1,65},{65,1},{2,66},{66,2},{3,67},{67,3},{4,68},{68... | collective-permute-start | bytes 98312 | tf_op jit(solution)/shard_map/basis_rows/ppermute | solution.py:29
  49.6 10.6 %collective-permute-start.1 = (f32[2,16,512]{2,1,0:T(8,128)S(1)}, f32[2,16,512]{2,1,0:T(8,128)S(1)}, u32[]{:S(2)}, u32[]{:S(2)}) collective-permute-start(f32[2,16,512]{2,1,0:T(8,128)S(1)} %bitcast_dynamic-update-slice_fusion.4), channel_id=1, source_target_pairs={{0,128},{128,256},{256,384},{384,0},{1,129},{129,257},{257,385},{3... | collective-permute-start | bytes 196616 | tf_op jit(solution)/shard_map/basis_rows/ppermute | solution.py:29
  52.7 7.5 %collective-permute-start.2 = (f32[2,16,512]{2,1,0:T(8,128)S(1)}, f32[2,16,512]{2,1,0:T(8,128)S(1)}, u32[]{:S(2)}, u32[]{:S(2)}) collective-permute-start(f32[2,16,512]{2,1,0:T(8,128)S(1)} %bitcast_dynamic-update-slice_fusion.4), channel_id=1, source_target_pairs={{0,256},{128,384},{256,0},{384,128},{1,257},{129,385},{257,1},{385... | collective-permute-start | bytes 196616 | tf_op jit(solution)/shard_map/basis_rows/ppermute | solution.py:29
  57.1 5.3 %collective-permute-start.3 = (f32[2,16,512]{2,1,0:T(8,128)S(1)}, f32[2,16,512]{2,1,0:T(8,128)S(1)}, u32[]{:S(2)}, u32[]{:S(2)}) collective-permute-start(f32[2,16,512]{2,1,0:T(8,128)S(1)} %bitcast_dynamic-update-slice_fusion.4), channel_id=1, source_target_pairs={{0,384},{128,0},{256,128},{384,256},{1,385},{129,1},{257,129},{385... | collective-permute-start | bytes 196616 | tf_op jit(solution)/shard_map/basis_rows/ppermute | solution.py:29

commit v6 on v5

--- a/solution.py
+++ b/solution.py
@@ -93,7 +93,7 @@
 def slab_sums(impedance, scales, entries, basis, members):
     rows = impedance.shape[1]
     columns = entries.shape[3]
-    chunks = 4
+    chunks = 2
     share = rows // members
     lanes = (basis.shape[0] // 2 // rows + 1) * columns
     vmem = pl.BlockSpec(memory_space=pltpu.VMEM)

time: 134 us -> 134 us (level)
  no operation moved by 1% of the time
where the time goes in v6:
time: 134 us; the launch traced here: 133 us
  blocking collectives  97.4 us (73%)
  starting transfers between devices  25.1 us (19%)
  Pallas kernels  6.39 us (5%)
  waiting for transfers between devices  2.89 us (2%)
    all_gather x1, blocking collectives, per_device(): along_z = lax.all_gather(krylov_block, 'z', axis=0)  32.1 us
    all_to_all x2, blocking collectives, per_device(): taken = lax.all_to_all(parts, PLANE, 0, 0, tiled=True)  30.4 us
    ppermute x4, starting transfers between devices, ring_gather(): arrived = lax.ppermute(block, axis, pairs) if step else block  20.9 us
    all_to_all x1, blocking collectives, spread(): return lax.all_to_all(copies, axes, 0, 0, tiled=True)  17.7 us
    all_to_all x1, blocking collectives, per_device(): sums = jnp.sum(lax.all_to_all(sums, COL, 0, 0, tiled=True), axis=0)  17.3 us
    all_to_all x1, starting transfers between devices, per_device(): entries = lax.all_to_all(copies_of(along_z, ys), 'y', 0, 0, tiled=True)  4.2 us
    pallas_call x1, Pallas kernels, slab_sums(): pl.pallas_call(functools.partial(slab_kernel, chunks), out_shape=jax.Shap...  3.87 us
    ppermute x4, waiting for transfers between devices, ring_gather(): arrived = lax.ppermute(block, axis, pairs) if step else block  2.89 us
  transfers between devices with their start and end apart: 5, of which 2 were waited for; matrix products, arithmetic and copies ran while one was open for 0% of the time, Pallas kernels for 0%

profile of v6, /device:TPU:1, one launch (start us, length us, event | category | flops | bytes accessed | tf_op | source)
XLA Modules:
  0.0 133.3 jit_solution(3251264999206503658)
XLA Ops:
  0.6 32.1 %all-gather = bf16[2048,128]{1,0:T(8,128)(2,1)S(1)} all-gather(bf16[128,128]{1,0:T(8,128)(2,1)} %param.6), channel_id=2, replica_groups=mesh['x'=4,'core'=2,'z'=16,'y'=4] {'z'}, dimensions={0}, use_global_device_ids=true | all-gather | bytes 557056 | tf_op jit(solution)/shard_map/entries_z/all_gather | solution.py:191
  32.7 1.4 %entries_y.1 = bf16[4,16,128,128]{3,2,1,0:T(8,128)(2,1)} custom-call(bf16[16,128,128]{2,1,0:T(8,128)(2,1)S(1)} %bitcast.25), custom_call_target="tpu_custom_call" | custom-call | tf_op jit(solution)/shard_map/entries_y/pallas_call | solution.py:51
  34.1 0.0 copy-start
  34.1 0.0 copy-start.1
  34.1 4.2 %all-to-all-start = ((bf16[4,16,128,128]{3,2,1,0:T(8,128)(2,1)}), bf16[4,16,128,128]{3,2,1,0:T(8,128)(2,1)S(1)}, u32[]{:S(2)}, u32[]{:S(2)}) async-start(bf16[4,16,128,128]{3,2,1,0:T(8,128)(2,1)} %entries_y.1), calls=%async_computation | async-start | bytes 4194304 | tf_op jit(solution)/shard_map/entries_y/all_to_all | solution.py:194
  38.3 0.0 copy-done
  38.3 10.4 %collective-permute-start = (f32[16,512]{1,0:T(8,128)S(1)}, f32[16,512]{1,0:T(8,128)S(1)}, u32[]{:S(2)}, u32[]{:S(2)}) collective-permute-start(f32[16,512]{1,0:T(8,128)S(1)} %copy-done), channel_id=1, source_target_pairs={{0,64},{64,0},{1,65},{65,1},{2,66},{66,2},{3,67},{67,3},{4,68},{68... | collective-permute-start | bytes 98312 | tf_op jit(solution)/shard_map/basis_rows/ppermute | solution.py:29
  48.8 0.8 collective-permute-done
  49.6 3.1 %collective-permute-start.1 = (f32[2,16,512]{2,1,0:T(8,128)S(1)}, f32[2,16,512]{2,1,0:T(8,128)S(1)}, u32[]{:S(2)}, u32[]{:S(2)}) collective-permute-start(f32[2,16,512]{2,1,0:T(8,128)S(1)} %bitcast_dynamic-update-slice_fusion.4), channel_id=1, source_target_pairs={{0,128},{128,256},{256,384},{384,0},{1,129},{129,257},{257,385},{3... | collective-permute-start | bytes 196616 | tf_op jit(solution)/shard_map/basis_rows/ppermute | solution.py:29
  52.7 4.4 %collective-permute-start.2 = (f32[2,16,512]{2,1,0:T(8,128)S(1)}, f32[2,16,512]{2,1,0:T(8,128)S(1)}, u32[]{:S(2)}, u32[]{:S(2)}) collective-permute-start(f32[2,16,512]{2,1,0:T(8,128)S(1)} %bitcast_dynamic-update-slice_fusion.4), channel_id=1, source_target_pairs={{0,256},{128,384},{256,0},{384,128},{1,257},{129,385},{257,1},{385... | collective-permute-start | bytes 196616 | tf_op jit(solution)/shard_map/basis_rows/ppermute | solution.py:29
  57.1 3.1 %collective-permute-start.3 = (f32[2,16,512]{2,1,0:T(8,128)S(1)}, f32[2,16,512]{2,1,0:T(8,128)S(1)}, u32[]{:S(2)}, u32[]{:S(2)}) collective-permute-start(f32[2,16,512]{2,1,0:T(8,128)S(1)} %bitcast_dynamic-update-slice_fusion.4), channel_id=1, source_target_pairs={{0,384},{128,0},{256,128},{384,256},{1,385},{129,1},{257,129},{385... | collective-permute-start | bytes 196616 | tf_op jit(solution)/shard_map/basis_rows/ppermute | solution.py:29
  60.2 0.0 collective-permute-done.1
  60.2 0.0 collective-permute-done.2
  60.2 2.1 %collective-permute-done.3 = f32[2,16,512]{2,1,0:T(8,128)S(1)} collective-permute-done((f32[2,16,512]{2,1,0:T(8,128)S(1)}, f32[2,16,512]{2,1,0:T(8,128)S(1)}, u32[]{:S(2)}, u32[]{:S(2)}) %collective-permute-start.3) | collective-permute-done | bytes 65568 | tf_op jit(solution)/shard_map/basis_rows/ppermute | solution.py:29
  62.4 0.1 copy.11.basis
  62.5 0.0 all-to-all-done.entries
  62.5 0.0 copy-done.1
  62.5 3.9 %slab.1 = f32[32,4,384]{2,1,0:T(4,128)S(1)} custom-call(bf16[2,128,8192]{2,1,0:T(8,128)(2,1)} %impedance.1, f32[128,16]{1,0:T(8,128)S(1)} %bitcast.26, bf16[4,16,128,128]{3,2,1,0:T(8,128)(2,1)S(1)} %all-to-all-done.entries, f32[512,128]{1,0:T(8,128)S(1)} %copy.11.basis), custom_call_target="tpu_custom_call" | custom-call | flops 536870912 | bytes 6291456 | tf_op jit(solution)/shard_map/slab/pallas_call | solution.py:100
  66.4 16.8 %all_to_all.29 = f32[32,4,384]{2,1,0:T(4,128)S(1)} all-to-all(f32[32,4,384]{2,1,0:T(4,128)S(1)} %slab.1), channel_id=1, replica_groups=mesh['x'=4,'core'=2,'z'=16,'y'=4] {'x','core','y'}, dimensions={0} | all-to-all | bytes 393216 | tf_op jit(solution)/shard_map/sums_plane/all_to_all | solution.py:206
  83.3 17.7 %all_to_all.30 = f32[16,4,256]{2,1,0:T(4,128)S(1)} all-to-all(f32[16,4,256]{2,1,0:T(4,128)S(1)} %broadcast_in_dim.59), channel_id=1, replica_groups=mesh['x'=4,'core'=2,'z'=16,'y'=4] {'z'}, dimensions={0} | all-to-all | bytes 131072 | tf_op jit(solution)/shard_map/coefficients_z/all_to_all | solution.py:20
  101.1 13.6 %all_to_all.31.taken = f32[32,4,384]{2,1,0:T(4,128)S(1)} all-to-all(f32[32,4,384]{2,1,0:T(4,128)S(1)} %pad_maximum_fusion), channel_id=1, replica_groups=mesh['x'=4,'core'=2,'z'=16,'y'=4] {'x','core','y'}, dimensions={0} | all-to-all | bytes 393216 | tf_op jit(solution)/shard_map/gather_plane/all_to_all | solution.py:215
  114.7 0.5 residual.1
  115.2 17.3 %all_to_all.32 = f32[64,1,128]{2,1,0:T(1,128)S(1)} all-to-all(f32[64,1,128]{2,1,0:T(1,128)S(1)} %bitcast.27), channel_id=1, replica_groups=mesh['x'=4,'core'=2,'z'=16,'y'=4] {'z','y'}, dimensions={0} | all-to-all | bytes 65536 | tf_op jit(solution)/shard_map/squares/all_to_all | solution.py:222
  132.5 0.1 reduce_sum.39
  132.6 0.7 scale.1
  (18 shorter events, 0.3 us)
Async XLA Ops:
  34.1 4.2 %copy-start = (f32[16,512]{1,0:T(8,128)S(1)}, f32[16,512]{1,0:T(8,128)}, u32[]{:S(2)}) copy-start(f32[16,512]{1,0:T(8,128)} %param.7) | copy-start | bytes 98308
  34.1 28.4 %copy-start.1 = (f32[8,16]{1,0:T(8,128)S(1)}, f32[8,16]{1,0:T(8,128)}, u32[]{:S(2)}) copy-start(f32[8,16]{1,0:T(8,128)} %param.5) | copy-start | bytes 1540
  34.1 28.4 %all-to-all-start = ((bf16[4,16,128,128]{3,2,1,0:T(8,128)(2,1)}), bf16[4,16,128,128]{3,2,1,0:T(8,128)(2,1)S(1)}, u32[]{:S(2)}, u32[]{:S(2)}) async-start(bf16[4,16,128,128]{3,2,1,0:T(8,128)(2,1)} %entries_y.1), calls=%async_computation | async-start | bytes 4194304 | tf_op jit(solution)/shard_map/entries_y/all_to_all | solution.py:194
  38.3 11.3 %collective-permute-start = (f32[16,512]{1,0:T(8,128)S(1)}, f32[16,512]{1,0:T(8,128)S(1)}, u32[]{:S(2)}, u32[]{:S(2)}) collective-permute-start(f32[16,512]{1,0:T(8,128)S(1)} %copy-done), channel_id=1, source_target_pairs={{0,64},{64,0},{1,65},{65,1},{2,66},{66,2},{3,67},{67,3},{4,68},{68... | collective-permute-start | bytes 98312 | tf_op jit(solution)/shard_map/basis_rows/ppermute | solution.py:29
  49.6 10.6 %collective-permute-start.1 = (f32[2,16,512]{2,1,0:T(8,128)S(1)}, f32[2,16,512]{2,1,0:T(8,128)S(1)}, u32[]{:S(2)}, u32[]{:S(2)}) collective-permute-start(f32[2,16,512]{2,1,0:T(8,128)S(1)} %bitcast_dynamic-update-slice_fusion.4), channel_id=1, source_target_pairs={{0,128},{128,256},{256,384},{384,0},{1,129},{129,257},{257,385},{3... | collective-permute-start | bytes 196616 | tf_op jit(solution)/shard_map/basis_rows/ppermute | solution.py:29
  52.7 7.5 %collective-permute-start.2 = (f32[2,16,512]{2,1,0:T(8,128)S(1)}, f32[2,16,512]{2,1,0:T(8,128)S(1)}, u32[]{:S(2)}, u32[]{:S(2)}) collective-permute-start(f32[2,16,512]{2,1,0:T(8,128)S(1)} %bitcast_dynamic-update-slice_fusion.4), channel_id=1, source_target_pairs={{0,256},{128,384},{256,0},{384,128},{1,257},{129,385},{257,1},{385... | collective-permute-start | bytes 196616 | tf_op jit(solution)/shard_map/basis_rows/ppermute | solution.py:29
  57.1 5.3 %collective-permute-start.3 = (f32[2,16,512]{2,1,0:T(8,128)S(1)}, f32[2,16,512]{2,1,0:T(8,128)S(1)}, u32[]{:S(2)}, u32[]{:S(2)}) collective-permute-start(f32[2,16,512]{2,1,0:T(8,128)S(1)} %bitcast_dynamic-update-slice_fusion.4), channel_id=1, source_target_pairs={{0,384},{128,0},{256,128},{384,256},{1,385},{129,1},{257,129},{385... | collective-permute-start | bytes 196616 | tf_op jit(solution)/shard_map/basis_rows/ppermute | solution.py:29
